TPU v7x, 32 devices: a whole 2x2x4 slice. The times are simulated.
32 devices in a mesh: freq: 4 (over z), tile: 8 (over y, x, core).
Axes of the slice: x: 2, y: 2, z: 4, core: 2. Of those that a mesh axis runs over, the one named last changes fastest.
Arguments:
- model_freq: bfloat16 [8, 16384, 384], P('freq', 'tile'), may hold values from -6 to 6
- recorded: bfloat16 [8, 16384, 384], P('freq', 'tile'), may hold values from -6 to 6
- v_factor: bfloat16 [8, 32, 32, 2, 64, 512], P('freq', 'tile'), may hold values from -0.25 to 0.25
- u_factor: bfloat16 [8, 32, 32, 2, 64, 512], P('freq', 'tile'), may hold values from -0.125 to 0.125
- tile_rank: int32 [8, 32, 32], P('freq', 'tile'), may hold values from 16 to 64
- tile_rows: int32 [32, 32], P('tile'), may hold values from 0 to 31, each once within a row
- omega: float32 [8], P('freq'), may hold values from 0.3 to 2.9
Outputs:
- lag_gradient: float32 [8, 16384, 192], P('freq', 'tile')
Inputs may be any that keep to these rules, and one draw needn't show every extreme that they name: Each row of tile_rows is a permutation of 0 to 31.
All inputs are finite; a program needn't handle non-finite values.
Results may differ from a plain program's by a relative error of at most 0.0037.
Values may be sent and summed in bfloat16 or wider, within the bound.
A program may use at most 256 MiB of HBM per device.

v0:
```python
import jax
import jax.numpy as jnp
from jax import lax
from jax.sharding import PartitionSpec as P

SOURCES = 192
LAG_DEV = 2


def per_device(model_freq, recorded, v_factor, u_factor, tile_rank, tile_rows, omega):
    half = SOURCES
    freq_local = v_factor.shape[0]
    block_local = v_factor.shape[1]
    tiles = v_factor.shape[2]
    rank_pad = v_factor.shape[4]
    width = v_factor.shape[5]
    select = (tile_rows[:, :, None] == jnp.arange(tiles, dtype=jnp.int32)[None, None, :]).astype(
        jnp.bfloat16
    )
    blocks = model_freq.reshape(freq_local, block_local, width, 2 * half)
    v_real = v_factor[:, :, :, 0]
    v_imag = v_factor[:, :, :, 1]
    first = jnp.einsum("fjkrt,fjts->fjkrs", v_real, blocks, preferred_element_type=jnp.float32)
    second = jnp.einsum("fjkrt,fjts->fjkrs", v_imag, blocks, preferred_element_type=jnp.float32)
    coeff = jnp.concatenate(
        [first[..., :half] - second[..., half:], first[..., half:] + second[..., :half]], -1
    )
    keep = (
        jnp.arange(rank_pad, dtype=jnp.int32)[None, None, None, :] < tile_rank[:, :, :, None]
    ).astype(jnp.float32)[..., None]
    coeff = (coeff * keep).astype(jnp.bfloat16)
    by_row = jnp.einsum(
        "jki,fjkrs->fjirs", select, coeff, preferred_element_type=jnp.float32
    ).astype(jnp.bfloat16)
    arrived = lax.all_to_all(by_row, "tile", split_axis=2, concat_axis=1, tiled=True)
    u_real = u_factor[:, :, :, 0]
    u_imag = u_factor[:, :, :, 1]
    upper = jnp.einsum("fijrt,fjirs->fits", u_real, arrived, preferred_element_type=jnp.float32)
    lower = jnp.einsum("fijrt,fjirs->fits", u_imag, arrived, preferred_element_type=jnp.float32)
    forward = jnp.concatenate(
        [upper[..., :half] - lower[..., half:], upper[..., half:] + lower[..., :half]], -1
    )
    observed = recorded.reshape(freq_local, block_local, width, 2 * half).astype(jnp.float32)
    resid = (forward - observed).astype(jnp.bfloat16)
    back_re = jnp.einsum("fijrt,fits->fijrs", u_real, resid, preferred_element_type=jnp.float32)
    back_im = jnp.einsum("fijrt,fits->fijrs", u_imag, resid, preferred_element_type=jnp.float32)
    back = jnp.concatenate(
        [back_re[..., :half] + back_im[..., half:], back_re[..., half:] - back_im[..., :half]], -1
    )
    back = back.astype(jnp.bfloat16)
    returned = lax.all_to_all(back, "tile", split_axis=2, concat_axis=1, tiled=True)
    slotted = jnp.einsum("jki,fijrs->fjkrs", select, returned, preferred_element_type=jnp.float32)
    slotted = (slotted * keep).astype(jnp.bfloat16)
    grad_a = jnp.einsum("fjkrt,fjkrs->fjts", v_real, slotted, preferred_element_type=jnp.float32)
    grad_b = jnp.einsum("fjkrt,fjkrs->fjts", v_imag, slotted, preferred_element_type=jnp.float32)
    grad = jnp.concatenate(
        [grad_a[..., :half] + grad_b[..., half:], grad_a[..., half:] - grad_b[..., :half]], -1
    )
    grad = grad.reshape(freq_local, block_local * width, 2 * half)
    groups = lax.axis_size("freq")
    freq_total = freq_local * groups
    lag_total = LAG_DEV * groups
    lag_axis = jnp.arange(lag_total, dtype=jnp.float32)
    phase = lag_axis[:, None] * omega[None, :]
    cosine = jnp.cos(phase)
    sine = jnp.sin(phase)
    partial_lags = jnp.einsum(
        "lf,fns->lns", cosine, grad[..., :half], precision=lax.Precision.HIGHEST
    )
    partial_lags = partial_lags - jnp.einsum(
        "lf,fns->lns", sine, grad[..., half:], precision=lax.Precision.HIGHEST
    )
    partial_lags = partial_lags * (2.0 / freq_total)
    return lax.psum_scatter(partial_lags, "freq", scatter_dimension=0, tiled=True)


def solution(mesh):
    placed = (
        P("freq", "tile", None),
        P("freq", "tile", None),
        P("freq", "tile", None, None, None, None),
        P("freq", "tile", None, None, None, None),
        P("freq", "tile", None),
        P("tile", None),
        P("freq"),
    )
    return jax.shard_map(
        per_device, mesh=mesh, in_specs=placed, out_specs=P("freq", "tile", None), check_vma=False
    )
```

profile of v0, /device:TPU:0, one launch (start us, length us, event | category | flops | bytes accessed | tf_op | source)
XLA Modules:
  0.0 945.4 jit_solution(7154293340415254309)
XLA Ops:
  6.5 0.0 copy-start
  6.5 1.9 copy-done
  8.4 16.9 %fusion.14 = f32[2,4,32,64,384]{4,3,2,1,0:T(8,128)} fusion(bf16[2,4,512,384,1]{3,2,4,1,0:T(8,128)(2,1)S(1)} %bitcast.130, bf16[2,4,32,2,64,512]{5,4,3,2,1,0:T(8,128)(2,1)} %param.9), kind=kOutput, calls=%fused_computation.20 | convolution fusion | flops 6442450944 | bytes 45088768 | tf_op jit(solution)/shard_map/fjkrt,fjts->fjkrs/dot_general | solution.py:24
  25.4 0.0 copy-start.8
  25.4 16.9 %fusion.18 = f32[2,4,32,64,384]{4,3,2,1,0:T(8,128)} fusion(bf16[2,4,512,384,1]{3,2,4,1,0:T(8,128)(2,1)S(1)} %bitcast.129, bf16[2,4,32,2,64,512]{5,4,3,2,1,0:T(8,128)(2,1)} %param.9), kind=kOutput, calls=%fused_computation.24 | convolution fusion | flops 6442450944 | bytes 45088768 | tf_op jit(solution)/shard_map/fjkrt,fjts->fjkrs/dot_general | solution.py:23
  42.3 0.0 copy-done.8
  42.3 0.1 fusion.58
  42.4 0.0 copy-start.4
  42.4 34.4 %slice_subtract_fusion.1 = (f32[2,4,32,64,192]{4,3,2,1,0:T(8,128)}, f32[2,4,32,64,192]{4,3,2,1,0:T(8,128)}) fusion(f32[2,4,32,64,384]{4,3,2,1,0:T(8,128)} %fusion.14, f32[2,4,32,64,384]{4,3,2,1,0:T(8,128)} %fusion.18), kind=kLoop, calls=%fused_computation.9 | loop fusion | flops 6291456 | bytes 75497472 | tf_op jit(solution)/shard_map/sub | solution.py:26
  76.9 0.0 copy-done.4
  76.9 0.0 copy-start.6
  76.9 18.3 %fusion = bf16[2,4,32,64,384]{4,3,2,1,0:T(8,128)(2,1)} fusion(f32[2,4,32,64,192]{4,3,2,1,0:T(8,128)} %get-tuple-element.8, f32[2,4,32,64,192]{4,3,2,1,0:T(8,128)} %get-tuple-element.7, f32[2,4,32,64]{3,2,1,0:T(8,128)S(1)} %fusion.58), kind=kLoop, calls=%fused_computation.1 | loop fusion | flops 18874368 | bytes 37814272 | tf_op jit(solution)/shard_map/convert_element_type | solution.py:31
  95.2 0.0 copy-done.6
  95.2 27.2 %convert_bitcast_fusion = bf16[2,4,32,64,384]{4,2,3,0,1:T(8,128)(2,1)} fusion(bf16[2,4,32,64,384]{4,3,2,1,0:T(8,128)(2,1)} %fusion, s32[4,32]{1,0:T(4,128)S(1)} %copy-done.6), kind=kOutput, calls=%fused_computation.39 | convolution fusion | flops 408948736 | bytes 25166336 | tf_op jit(solution)/shard_map/jki,fjkrs->fjirs/dot_general | solution.py:32
  122.4 12.9 %copy.40 = bf16[2,4,32,64,384]{4,3,0,1,2:T(8,128)(2,1)} copy(bf16[2,4,32,64,384]{4,2,3,0,1:T(8,128)(2,1)} %convert_bitcast_fusion) | data formatting | bytes 25165824 | tf_op jit(solution)/shard_map/convert_element_type | solution.py:34
  135.3 0.0 copy-start.3
  135.3 5.6 all-to-all-start
  140.9 0.0 reduce-scatter.2.cloned.1.call-start
  141.0 0.0 copy-done.3
  141.0 3.8 copy.44
  144.8 135.8 %all-to-all-done = bf16[2,4,32,64,384]{4,3,0,1,2:T(8,128)(2,1)} async-done(((bf16[2,4,32,64,384]{4,3,0,1,2:T(8,128)(2,1)}), bf16[2,4,32,64,384]{4,3,0,1,2:T(8,128)(2,1)}, u32[]{:S(2)}, u32[]{:S(2)}) %all-to-all-start) | async-done | bytes 12582944 | tf_op jit(solution)/shard_map/all_to_all | solution.py:35
  280.6 10.9 %copy.41 = bf16[2,4,8,4,64,384]{5,4,1,2,3,0:T(8,128)(2,1)} copy(bf16[2,4,8,4,64,384]{5,4,0,1,3,2:T(8,128)(2,1)} %bitcast.10) | data formatting | bytes 25165824 | tf_op jit(solution)/shard_map/all_to_all | solution.py:35
  291.5 14.5 %fusion.42 = f32[2,4,512,384]{2,3,1,0:T(8,128)} fusion(bf16[2,32,4,64,384]{4,3,1,2,0:T(8,128)(2,1)} %bitcast.134, bf16[2,4,32,2,64,512]{5,4,3,2,1,0:T(8,128)(2,1)} %param.10), kind=kOutput, calls=%fused_computation.50 | convolution fusion | flops 6442450944 | bytes 35651584 | tf_op jit(solution)/shard_map/fijrt,fjirs->fits/dot_general | solution.py:38
  306.0 14.5 %fusion.45 = f32[2,4,512,384]{2,3,1,0:T(8,128)} fusion(bf16[2,32,4,64,384]{4,3,1,2,0:T(8,128)(2,1)} %bitcast.135, bf16[2,4,32,2,64,512]{5,4,3,2,1,0:T(8,128)(2,1)} %param.10), kind=kOutput, calls=%fused_computation.51 | convolution fusion | flops 6442450944 | bytes 35651584 | tf_op jit(solution)/shard_map/fijrt,fjirs->fits/dot_general | solution.py:39
  320.6 6.4 slice_subtract_fusion.3
  327.0 4.0 fusion.41
  331.1 17.4 %fusion.30 = f32[2,4,32,64,384]{4,3,2,1,0:T(8,128)} fusion(bf16[2,4,512,384,1]{2,3,4,1,0:T(8,128)(2,1)S(1)} %fusion.41, bf16[2,4,32,2,64,512]{5,4,3,2,1,0:T(8,128)(2,1)} %param.10), kind=kOutput, calls=%fused_computation.40 | convolution fusion | flops 6442450944 | bytes 45088768 | tf_op jit(solution)/shard_map/fijrt,fits->fijrs/dot_general | solution.py:45
  348.5 17.0 %fusion.33 = f32[2,4,32,64,384]{4,3,2,1,0:T(8,128)} fusion(bf16[2,4,512,384,1]{2,3,4,1,0:T(8,128)(2,1)S(1)} %fusion.41, bf16[2,4,32,2,64,512]{5,4,3,2,1,0:T(8,128)(2,1)} %param.10), kind=kOutput, calls=%fused_computation.41 | convolution fusion | flops 6442450944 | bytes 45088768 | tf_op jit(solution)/shard_map/fijrt,fits->fijrs/dot_general | solution.py:46
  365.4 29.0 %fusion.3 = (bf16[2,4,32,64,192]{4,3,2,1,0:T(8,128)(2,1)}, bf16[2,4,32,64,192]{4,3,2,1,0:T(8,128)(2,1)}) fusion(f32[2,4,32,64,384]{4,3,2,1,0:T(8,128)} %fusion.33, f32[2,4,32,64,384]{4,3,2,1,0:T(8,128)} %fusion.30), kind=kLoop, calls=%fused_computation.7 | loop fusion | flops 12582912 | bytes 62914560 | tf_op jit(solution)/shard_map/convert.1
  394.5 10.3 %pad_maximum_fusion = bf16[2,4,32,64,384]{4,3,2,1,0:T(8,128)(2,1)S(1)} fusion(bf16[2,4,32,64,192]{4,3,2,1,0:T(8,128)(2,1)} %get-tuple-element.6, bf16[2,4,32,64,192]{4,3,2,1,0:T(8,128)(2,1)} %get-tuple-element.5), kind=kLoop, calls=%fused_computation.34 | loop fusion | flops 25165824 | bytes 25165824 | tf_op jit(solution)/shard_map/concatenate | solution.py:47
  404.8 3.2 copy.47
  408.0 141.8 %all_to_all.36 = bf16[2,4,32,64,384]{4,3,1,0,2:T(8,128)(2,1)S(1)} all-to-all(bf16[2,4,32,64,384]{4,3,1,0,2:T(8,128)(2,1)S(1)} %copy.47), channel_id=1, replica_groups=mesh['freq'=4,'tile'=8] {'tile'}, dimensions={2} | all-to-all | bytes 25165824 | tf_op jit(solution)/shard_map/all_to_all | solution.py:51
  549.8 9.7 %copy.87 = bf16[2,4,8,4,64,384]{5,1,2,4,0,3:T(4,128)(2,1)} copy(bf16[2,4,8,4,64,384]{5,4,1,0,3,2:T(8,128)(2,1)S(1)} %bitcast.131) | data formatting | bytes 25165824 | tf_op jit(solution)/shard_map/all_to_all | solution.py:51
  559.5 0.0 copy-start.7
  559.5 20.4 %all_to_all.33 = bf16[2,32,4,64,384]{4,1,3,0,2:T(8,128)(2,1)} reshape(bf16[2,8,4,4,64,384]{5,2,1,4,0,3:T(4,128)(2,1)} %bitcast.132) | data formatting | bytes 25165824 | tf_op jit(solution)/shard_map/all_to_all | solution.py:51
  579.9 0.0 copy-done.7
  579.9 0.0 copy-start.5
  579.9 12.9 %fusion.60 = f32[4,2,64,384,32]{3,4,2,1,0:T(8,128)} fusion(bf16[2,32,4,64,384]{4,1,3,0,2:T(8,128)(2,1)} %all_to_all.33, s32[4,32]{1,0:T(4,128)S(1)} %copy-done.7), kind=kOutput, calls=%fused_computation.58 | convolution fusion | flops 402657280 | bytes 37749248 | tf_op jit(solution)/shard_map/jki,fijrs->fjkrs/dot_general | solution.py:52
  592.8 0.0 copy-done.5
  592.8 28.0 %fusion.48 = f32[2,4,512,384]{2,3,1,0:T(8,128)S(1)} fusion(bf16[2,4,32,2,64,512]{5,4,3,2,1,0:T(8,128)(2,1)} %param.9, f32[4,2,64,384,32]{3,4,2,1,0:T(8,128)} %fusion.60, f32[2,4,32,64]{3,2,1,0:T(8,128)S(1)} %copy-done.5), kind=kOutput, calls=%fused_computation.52 | convolution fusion | flops 6455033856 | bytes 48300032 | tf_op jit(solution)/shard_map/fjkrt,fjkrs->fjts/dot_general | solution.py:54
  620.9 28.3 %fusion.53 = f32[2,4,512,384]{2,3,1,0:T(8,128)S(1)} fusion(bf16[2,4,32,2,64,512]{5,4,3,2,1,0:T(8,128)(2,1)} %param.9, f32[4,2,64,384,32]{3,4,2,1,0:T(8,128)} %fusion.60, f32[2,4,32,64]{3,2,1,0:T(8,128)S(1)} %copy-done.5), kind=kOutput, calls=%fused_computation.53 | convolution fusion | flops 6455033856 | bytes 48300032 | tf_op jit(solution)/shard_map/fjkrt,fjkrs->fjts/dot_general | solution.py:55
  649.1 1.6 slice_add_fusion.2
  650.7 3.3 pad_maximum_fusion.1
  654.0 6.6 copy.50
  660.6 0.0 copy-start.9
  660.6 8.0 fusion.72
  668.6 4.9 copy.73
  673.6 6.0 copy.74
  679.5 0.0 copy-done.9
  679.5 0.0 copy-start.2
  679.5 14.0 %fusion.66 = f32[8,2048,192]{1,0,2:T(8,128)S(1)} fusion(f32[2,2048,192]{1,0,2:T(2,128)S(1)} %copy.73, f32[2]{0:T(128)S(1)} %copy-done.9), kind=kOutput, calls=%fused_computation.62 | convolution fusion | flops 75497488 | bytes 15728648 | tf_op jit(solution)/shard_map/lf,fns->lns/dot_general | solution.py:67
  693.5 0.0 copy-done.2
  693.6 16.1 %subtract_multiply_fusion = f32[8,2048,192]{1,0,2:T(8,128)} fusion(f32[8,2048,192]{1,0,2:T(8,128)S(1)} %fusion.66, f32[2,2048,192]{1,0,2:T(2,128)S(1)} %copy-done.2, f32[2]{0:T(128)S(1)} %copy-done.9), kind=kOutput, calls=%fused_computation.38 | convolution fusion | flops 81788944 | bytes 28311560 | tf_op jit(solution)/shard_map/lf,fns->lns/dot_general | solution.py:70
  709.7 0.0 copy-start.1
  709.7 16.5 %copy.53 = f32[8,2048,192]{1,2,0:T(8,128)} copy(f32[8,2048,192]{1,0,2:T(8,128)} %subtract_multiply_fusion) | data formatting | bytes 25165824 | tf_op jit(solution)/shard_map/mul | solution.py:73
  726.2 0.0 reduce-scatter.2.cloned.1.call-update
  726.2 212.2 %reduce-scatter.2.cloned.1.call-done = f32[2,2048,192]{1,2,0:T(8,128)} async-done(((f32[8,2048,192]{1,2,0:T(8,128)}), f32[2,2048,192]{1,2,0:T(8,128)}) %reduce-scatter.2.cloned.1.call-update) | async-done | bytes 3145744 | tf_op jit(solution)/shard_map/reduce_scatter | solution.py:74
  938.4 0.0 copy-done.1
Async XLA Ops:
  6.5 1.9 copy-start
  25.4 17.0 %copy-start.8 = (s32[2,4,32]{2,1,0:T(4,128)S(1)}, s32[2,4,32]{2,1,0:T(4,128)}, u32[]{:S(2)}) copy-start(s32[2,4,32]{2,1,0:T(4,128)} %param.11) | copy-start | bytes 3076
  42.4 34.4 %copy-start.4 = (f32[2,4,32,64]{3,2,1,0:T(8,128)}, f32[2,4,32,64]{3,2,1,0:T(8,128)S(1)}, u32[]{:S(2)}) copy-start(f32[2,4,32,64]{3,2,1,0:T(8,128)S(1)} %fusion.58) | copy-start | bytes 196612
  76.9 18.3 %copy-start.6 = (s32[4,32]{1,0:T(4,128)S(1)}, s32[4,32]{1,0:T(4,128)}, u32[]{:S(2)}) copy-start(s32[4,32]{1,0:T(4,128)} %param.12) | copy-start | bytes 1540
  135.3 5.7 copy-start.3
  135.3 145.3 %all-to-all-start = ((bf16[2,4,32,64,384]{4,3,0,1,2:T(8,128)(2,1)}), bf16[2,4,32,64,384]{4,3,0,1,2:T(8,128)(2,1)}, u32[]{:S(2)}, u32[]{:S(2)}) async-start(bf16[2,4,32,64,384]{4,3,0,1,2:T(8,128)(2,1)} %copy.40), calls=%async_computation | async-start | bytes 25165824 | tf_op jit(solution)/shard_map/all_to_all | solution.py:35
  140.9 797.4 %reduce-scatter.2.cloned.1.call-start = ((), (), s32[]{:S(2)}) async-start(), calls=%async_computation.3 | async-start | bytes 15728640 | tf_op jit(solution)/shard_map/reduce_scatter | solution.py:74
  559.5 20.4 %copy-start.7 = (s32[4,32]{1,0:T(4,128)S(1)}, s32[4,32]{1,0:T(4,128)}, u32[]{:S(2)}) copy-start(s32[4,32]{1,0:T(4,128)} %param.12) | copy-start | bytes 1540
  579.9 12.9 %copy-start.5 = (f32[2,4,32,64]{3,2,1,0:T(8,128)S(1)}, f32[2,4,32,64]{3,2,1,0:T(8,128)}, u32[]{:S(2)}) copy-start(f32[2,4,32,64]{3,2,1,0:T(8,128)} %copy-done.4) | copy-start | bytes 196612
  660.6 18.9 %copy-start.9 = (f32[2]{0:T(128)S(1)}, f32[2]{0:T(128)}, u32[]{:S(2)}) copy-start(f32[2]{0:T(128)} %param.13) | copy-start | bytes 28
  679.5 14.0 %copy-start.2 = (f32[2,2048,192]{1,0,2:T(2,128)S(1)}, f32[2,2048,192]{1,0,2:T(2,128)}, u32[]{:S(2)}) copy-start(f32[2,2048,192]{1,0,2:T(2,128)} %copy.74) | copy-start | bytes 9437188
  709.7 228.7 %copy-start.1 = (bf16[2,2048,384]{2,1,0:T(8,128)(2,1)S(1)}, bf16[2,2048,384]{2,1,0:T(8,128)(2,1)}, u32[]{:S(2)}) copy-start(bf16[2,2048,384]{2,1,0:T(8,128)(2,1)} %param.7) | copy-start | bytes 9437188
Sparse Core Ops, SparseCore 0:
  726.3 211.9 reduce-scatter.1
where the time goes:
time: 949 us; the launch traced here: 945 us
  waiting for transfers between devices  348 us (37%)
  matrix products  224 us (24%)
  blocking collectives  142 us (15%)
  other arithmetic  108 us (11%)
  local copies, waits for them, and re-layouts  105 us (11%)
  between operations  13.7 us (1%)
    reduce_scatter x1, waiting for transfers between devices, per_device(): lax.psum_scatter(partial_lags, 'freq', scatter_dimension=0, tiled=True)  212 us
    all_to_all x1, blocking collectives, per_device(): lax.all_to_all(back, 'tile', split_axis=2, concat_axis=1, tiled=True)  142 us
    all_to_all x1, waiting for transfers between devices, per_device(): lax.all_to_all(by_row, 'tile', split_axis=2, concat_axis=1, tiled=True)  136 us
    sub x1, other arithmetic, per_device(): first[..., :half] - second[..., half:]  34.4 us
    all_to_all x2, local copies, waits for them, and re-layouts, per_device(): lax.all_to_all(back, 'tile', split_axis=2, concat_axis=1, tiled=True)  30.1 us
    another operation x1, other arithmetic  29 us
    dot_general x1, matrix products, per_device(): jnp.einsum('fjkrt,fjkrs->fjts', v_imag, slotted, preferred_element_type=j...  28.3 us
    dot_general x1, matrix products, per_device(): jnp.einsum('fjkrt,fjkrs->fjts', v_real, slotted, preferred_element_type=j...  28 us
  transfers between devices with their start and end apart: 2, of which 2 were waited for; matrix products, arithmetic and copies ran while one was open for 0% of the time, Pallas kernels for 0%

commit v1 on v0

v1 whole, which is shorter than its diff:
```python
import functools

import jax
import jax.numpy as jnp
from jax import lax
from jax.experimental import pallas as pl
from jax.experimental.pallas import tpu as pltpu
from jax.sharding import PartitionSpec as P

VMEM_BYTES = 44 * 1024 * 1024
GROUP = 8


def turn(block):
    half = block.shape[-1] // 2
    return jnp.concatenate([-block[:, half:], block[:, :half]], -1)


def turn_back(block):
    half = block.shape[-1] // 2
    return jnp.concatenate([block[:, half:], -block[:, :half]], -1)


def dot(left, right):
    return lax.dot_general(left, right, (((1,), (0,)), ((), ())), preferred_element_type=jnp.float32)


def dot_rows(left, right):
    return lax.dot_general(left, right, (((0,), (0,)), ((), ())), preferred_element_type=jnp.float32)


def part_of(ref, lead, start, count, part):
    rank, width = ref.shape[-2], ref.shape[-1]
    return ref[(*lead, pl.ds(start, count), part)].reshape(count * rank, width)


def coeff_body(freq, rows_ref, rank_ref, v_ref, x_ref, out_ref, x2_ref):
    block = pl.program_id(0)
    tiles, rank, cols = v_ref.shape[2], v_ref.shape[4], x_ref.shape[-1]
    group = min(GROUP, tiles)
    x2_ref[...] = turn(x_ref[0, 0])
    row = lax.broadcasted_iota(jnp.int32, (rank, cols), 0)

    @pl.loop(0, tiles // group)
    def _(step):
        first = step * group
        total = dot(part_of(v_ref, (0, 0), first, group, 0), x_ref[0, 0])
        total += dot(part_of(v_ref, (0, 0), first, group, 1), x2_ref[...])
        for t in range(group):
            slot = first + t
            kept = row < rank_ref[freq, block, slot]
            tile = jnp.where(kept, total[t * rank : (t + 1) * rank], 0.0)
            out_ref[rows_ref[block, slot], 0] = tile.astype(out_ref.dtype)


def coeff_call(freq, tile_rows, tile_rank, v_factor, blocks):
    _, own, tiles, _, rank, width = v_factor.shape
    cols = blocks.shape[-1]
    return pl.pallas_call(
        functools.partial(coeff_body, freq),
        grid_spec=pltpu.PrefetchScalarGridSpec(
            num_scalar_prefetch=2,
            grid=(own,),
            in_specs=[
                pl.BlockSpec((1, 1, tiles, 2, rank, width), lambda j, *_: (freq, j, 0, 0, 0, 0)),
                pl.BlockSpec((1, 1, width, cols), lambda j, *_: (freq, j, 0, 0)),
            ],
            out_specs=pl.BlockSpec((tiles, 1, rank, cols), lambda j, *_: (0, j, 0, 0)),
            scratch_shapes=[pltpu.VMEM((width, cols), jnp.bfloat16)],
        ),
        out_shape=jax.ShapeDtypeStruct((tiles, own, rank, cols), jnp.bfloat16),
        compiler_params=pltpu.CompilerParams(vmem_limit_bytes=VMEM_BYTES),
        cost_estimate=pl.CostEstimate(
            flops=4 * own * tiles * rank * width * cols,
            bytes_accessed=own * tiles * rank * (4 * width + 2 * cols),
            transcendentals=0,
        ),
        name="coeff",
    )(tile_rows, tile_rank, v_factor, blocks)


def middle_body(u_ref, c_ref, seen_ref, *rest):
    outs, (acc_ref, resid_ref, resid2_ref) = rest[:-3], rest[-3:]
    sources, own, rank, cols = c_ref.shape[0], c_ref.shape[2], c_ref.shape[3], c_ref.shape[4]
    acc_ref[...] = -seen_ref[0, 0].astype(jnp.float32)
    per = max(1, GROUP // own)

    @pl.loop(0, sources // per)
    def _(step):
        first = step * per
        coeff = c_ref[pl.ds(first, per), 0].reshape(per * own * rank, cols)
        acc_ref[...] += dot_rows(part_of(u_ref, (0, 0), first * own, per * own, 0), coeff) + dot_rows(
            part_of(u_ref, (0, 0), first * own, per * own, 1), turn(coeff)
        )

    resid = acc_ref[...].astype(jnp.bfloat16)
    resid_ref[...] = resid
    resid2_ref[...] = turn_back(resid)

    @pl.loop(0, sources // per)
    def _(step):
        first = step * per
        total = dot(part_of(u_ref, (0, 0), first * own, per * own, 0), resid_ref[...])
        total += dot(part_of(u_ref, (0, 0), first * own, per * own, 1), resid2_ref[...])
        back = total.astype(jnp.bfloat16).reshape(per, own, rank, cols)
        for d in range(per):
            for j in range(own):
                outs[j][first + d, 0] = back[d, j]


def middle_call(freq, u_factor, arrived, seen):
    _, own, tiles, _, rank, width = u_factor.shape
    sources = tiles // own
    cols = seen.shape[-1]
    return pl.pallas_call(
        middle_body,
        grid=(own,),
        in_specs=[
            pl.BlockSpec((1, 1, tiles, 2, rank, width), lambda i: (freq, i, 0, 0, 0, 0)),
            pl.BlockSpec((sources, 1, own, rank, cols), lambda i: (0, i, 0, 0, 0)),
            pl.BlockSpec((1, 1, width, cols), lambda i: (freq, i, 0, 0)),
        ],
        out_specs=[pl.BlockSpec((sources, 1, rank, cols), lambda i: (0, i, 0, 0))] * own,
        out_shape=[jax.ShapeDtypeStruct((sources, own, rank, cols), jnp.bfloat16)] * own,
        scratch_shapes=[
            pltpu.VMEM((width, cols), jnp.float32),
            pltpu.VMEM((width, cols), jnp.bfloat16),
            pltpu.VMEM((width, cols), jnp.bfloat16),
        ],
        compiler_params=pltpu.CompilerParams(vmem_limit_bytes=VMEM_BYTES),
        cost_estimate=pl.CostEstimate(
            flops=8 * own * tiles * rank * width * cols,
            bytes_accessed=own * tiles * rank * (4 * width + 4 * cols),
            transcendentals=0,
        ),
        name="middle",
    )(u_factor, arrived.reshape(sources, own, own, rank, cols), seen)


def grad_body(block, freqs, rows_ref, rank_ref, cos_ref, sin_ref, v_ref, *rest):
    backs, out_ref, acc_ref = rest[:freqs], rest[freqs], rest[freqs + 1]
    freq = pl.program_id(0)
    tiles, rank = v_ref.shape[2], v_ref.shape[4]
    cols = acc_ref.shape[1]
    half = cols // 2
    group = min(GROUP, tiles)
    row = lax.broadcasted_iota(jnp.int32, (rank, cols), 0)
    for f in range(freqs):

        @pl.when(freq == f)
        def _():
            acc_ref[f] = jnp.zeros(acc_ref.shape[1:], jnp.float32)

            @pl.loop(0, tiles // group)
            def _(step):
                first = step * group
                picked = []
                for t in range(group):
                    slot = first + t
                    kept = row < rank_ref[f, block, slot]
                    tile = backs[f][rows_ref[block, slot]]
                    picked.append(jnp.where(kept, tile, jnp.zeros_like(tile)))
                back = jnp.concatenate(picked, 0)
                acc_ref[f] += dot_rows(back, part_of(v_ref, (0, 0), first, group, 0)) + dot_rows(
                    turn_back(back), part_of(v_ref, (0, 0), first, group, 1)
                )

    @pl.when(freq == freqs - 1)
    def _():
        chunk = 16
        pairs = out_ref.shape[1]

        @pl.loop(0, half // chunk)
        def _(step):
            here = pl.ds(step * chunk, chunk)
            real = [acc_ref[f, here] for f in range(freqs)]
            imag = [acc_ref[f, pl.ds(half + step * chunk, chunk)] for f in range(freqs)]
            for lag in range(cos_ref.shape[0]):
                total = real[0] * cos_ref[lag, 0] - imag[0] * sin_ref[lag, 0]
                for f in range(1, freqs):
                    total += real[f] * cos_ref[lag, f] - imag[f] * sin_ref[lag, f]
                out_ref[lag // pairs, lag % pairs, here] = total.astype(out_ref.dtype)


def grad_call(block, tile_rows, tile_rank, cosine, sine, v_factor, backs, groups):
    freqs, own, tiles, _, rank, width = v_factor.shape
    cols = backs[0].shape[-1]
    lags = cosine.shape[0]
    whole = pl.BlockSpec((tiles, rank, cols), lambda f, *_: (0, 0, 0))
    return pl.pallas_call(
        functools.partial(grad_body, block, freqs),
        grid_spec=pltpu.PrefetchScalarGridSpec(
            num_scalar_prefetch=4,
            grid=(freqs,),
            in_specs=[
                pl.BlockSpec((1, 1, tiles, 2, rank, width), lambda f, *_: (f, block, 0, 0, 0, 0)),
                *[whole] * freqs,
            ],
            out_specs=pl.BlockSpec((groups, lags // groups, cols // 2, width), lambda f, *_: (0, 0, 0, 0)),
            scratch_shapes=[pltpu.VMEM((freqs, cols, width), jnp.float32)],
        ),
        out_shape=jax.ShapeDtypeStruct((groups, lags // groups, cols // 2, width), jnp.bfloat16),
        compiler_params=pltpu.CompilerParams(vmem_limit_bytes=VMEM_BYTES),
        cost_estimate=pl.CostEstimate(
            flops=4 * freqs * tiles * rank * width * cols,
            bytes_accessed=freqs * tiles * rank * (4 * width + 2 * cols),
            transcendentals=0,
        ),
        name="grad",
    )(tile_rows, tile_rank, cosine, sine, v_factor, *backs)


def exchange(array, axis):
    return lax.all_to_all(array, axis, split_axis=0, concat_axis=0, tiled=True)


def per_device(model_freq, recorded, v_factor, u_factor, tile_rank, tile_rows, omega):
    freqs, own, tiles, _, rank, width = v_factor.shape
    cols = model_freq.shape[-1]
    groups = lax.axis_size("freq")
    blocks = model_freq.reshape(freqs, own, width, cols)
    seen = recorded.reshape(freqs, own, width, cols)
    total = freqs * groups
    phase = jnp.arange(total, dtype=jnp.float32)[:, None] * omega[None, :]
    cosine = jnp.cos(phase) * (2.0 / total)
    sine = jnp.sin(phase) * (2.0 / total)

    arrived = []
    for f in range(freqs):
        arrived.append(exchange(coeff_call(f, tile_rows, tile_rank, v_factor, blocks), "tile"))
    backs = [middle_call(f, u_factor, arrived[f], seen) for f in range(freqs)]
    parts = []
    for j in range(own):
        returned = [
            exchange(backs[f][j].reshape(tiles, rank, cols), "tile").reshape(tiles, rank, cols) for f in range(freqs)
        ]
        shares = grad_call(j, tile_rows, tile_rank, cosine, sine, v_factor, returned, groups)
        parts.append(jnp.sum(exchange(shares, "freq").astype(jnp.float32), 0))
    return jnp.swapaxes(jnp.concatenate(parts, 2), 1, 2)


def solution(mesh):
    placed = (
        P("freq", "tile", None),
        P("freq", "tile", None),
        P("freq", "tile", None, None, None, None),
        P("freq", "tile", None, None, None, None),
        P("freq", "tile", None),
        P("tile", None),
        P("freq"),
    )
    return jax.shard_map(
        per_device, mesh=mesh, in_specs=placed, out_specs=P("freq", "tile", None), check_vma=False
    )
```

time: 949 us -> 554 us (0.58)
  matrix products: 224 us -> 0 us
  waiting for transfers between devices: 348 us -> 192 us
  Pallas kernels: 0 us -> 136 us
  other arithmetic: 108 us -> 8.25 us
  local copies, waits for them, and re-layouts: 105 us -> 34.3 us
  starting transfers between devices: 5.66 us -> 35.6 us
  between operations: 13.7 us -> 0.28 us
    dot_general x12 -> x0, matrix products: 224 us -> none  [the longest x1 28.3 us: per_device(): jnp.einsum('fjkrt,fjkrs->fjts', v_imag, slotted, preferred_element_type=j...]
    reduce_scatter x1 -> x0, waiting for transfers between devices: 212 us -> none  [per_device(): lax.psum_scatter(partial_lags, 'freq', scatter_dimension=0, tiled=True)]
    pallas_call x0 -> x8, Pallas kernels: none -> 136 us  [the longest x2 61.6 us: middle_call(): pl.pallas_call(middle_body, grid=(own,), in_specs=[pl.BlockSpec((1, 1, ti...]
    all_to_all x1 -> x8, waiting for transfers between devices: 136 us -> 192 us  [exchange(): return lax.all_to_all(array, axis, split_axis=0, concat_axis=0, tiled=True)]
    all_to_all x3 -> x0, local copies, waits for them, and re-layouts: 41 us -> none  [the longest x2 30.1 us: per_device(): lax.all_to_all(back, 'tile', split_axis=2, concat_axis=1, tiled=True)]
    sub x2 -> x0, other arithmetic: 40.9 us -> none  [the longest x1 34.4 us: per_device(): first[..., :half] - second[..., half:]]
    all_to_all x1 -> x8, starting transfers between devices: 5.62 us -> 35.6 us  [exchange(): return lax.all_to_all(array, axis, split_axis=0, concat_axis=0, tiled=True)]
    another operation x1 -> x0, other arithmetic: 29 us -> none
  transfers between devices with their start and end apart: 2 -> 8, of which waited for: 2 -> 7; matrix products, arithmetic and copies ran while one was open for 0% -> 1% of each run, Pallas kernels for 0% -> 22%
where the time goes in v1:
time: 554 us; the launch traced here: 552 us
  waiting for transfers between devices  192 us (35%)
  blocking collectives  146 us (26%)
  Pallas kernels  136 us (25%)
  starting transfers between devices  35.6 us (6%)
  local copies, waits for them, and re-layouts  34.3 us (6%)
  other arithmetic  8.25 us (1%)
    all_to_all x8, waiting for transfers between devices, exchange(): return lax.all_to_all(array, axis, split_axis=0, concat_axis=0, tiled=True)  192 us
    all_to_all x6, blocking collectives, exchange(): return lax.all_to_all(array, axis, split_axis=0, concat_axis=0, tiled=True)  146 us
    pallas_call x2, Pallas kernels, middle_call(): pl.pallas_call(middle_body, grid=(own,), in_specs=[pl.BlockSpec((1, 1, ti...  61.6 us
    pallas_call x4, Pallas kernels, grad_call(): pl.pallas_call(functools.partial(grad_body, block, freqs), grid_spec=pltp...  42.3 us
    all_to_all x8, starting transfers between devices, exchange(): return lax.all_to_all(array, axis, split_axis=0, concat_axis=0, tiled=True)  35.6 us
    unnamed x68, local copies, waits for them, and re-layouts  34.3 us
    pallas_call x2, Pallas kernels, coeff_call(): pl.pallas_call(functools.partial(coeff_body, freq), grid_spec=pltpu.Prefe...  31.9 us
  transfers between devices with their start and end apart: 8, of which 7 were waited for; matrix products, arithmetic and copies ran while one was open for 1% of the time, Pallas kernels for 22%

profile of v1, /device:TPU:0, one launch (start us, length us, event | category | flops | bytes accessed | tf_op | source)
XLA Modules:
  0.0 551.7 jit_solution(60249517291727255)
XLA Ops:
  0.0 1.9 copy-done.2
  1.9 0.7 copy-done.26
  2.6 0.7 copy-done.28
  3.3 16.0 %coeff.2 = bf16[32,4,64,384]{3,2,1,0:T(8,128)(2,1)S(1)} custom-call(s32[4,32]{1,0:T(4,128)S(1)} %copy-done.28, s32[2,4,32]{2,1,0:T(4,128)S(1)} %copy-done.26, bf16[2,4,32,2,64,512]{5,4,3,2,1,0:T(8,128)(2,1)} %v_ref.11, bf16[2,4,512,384]{3,2,1,0:T(8,128)(2,1)S(1)} %bitcast.14), custom_call_target="tpu_custom_call" | custom-call | flops 6442450944 | bytes 23068672 | tf_op jit(solution)/shard_map/coeff/pallas_call | solution.py:59
  19.2 2.6 copy-done.1
  21.9 5.4 all-to-all-start
  27.3 16.0 %coeff.3 = bf16[32,4,64,384]{3,2,1,0:T(8,128)(2,1)S(1)} custom-call(s32[4,32]{1,0:T(4,128)S(1)} %copy-done.29, s32[2,4,32]{2,1,0:T(4,128)S(1)} %copy-done.27, bf16[2,4,32,2,64,512]{5,4,3,2,1,0:T(8,128)(2,1)} %v_ref.11, bf16[2,4,512,384]{3,2,1,0:T(8,128)(2,1)S(1)} %bitcast.15), custom_call_target="tpu_custom_call" | custom-call | flops 6442450944 | bytes 23068672 | tf_op jit(solution)/shard_map/coeff/pallas_call | solution.py:59
  43.3 2.6 copy-done
  45.9 53.2 %all-to-all-done = bf16[32,4,64,384]{3,2,1,0:T(8,128)(2,1)} async-done(((bf16[32,4,64,384]{3,2,1,0:T(8,128)(2,1)}), bf16[32,4,64,384]{3,2,1,0:T(8,128)(2,1)}, u32[]{:S(2)}, u32[]{:S(2)}) %all-to-all-start) | async-done | bytes 6291488 | tf_op jit(solution)/shard_map/all_to_all | solution.py:214
  99.1 4.7 all-to-all-start.2
  103.9 0.0 copy-start.30
  103.9 1.9 copy-done.30
  105.8 30.8 %middle.2 = (bf16[8,4,64,384]{3,2,1,0:T(8,128)(2,1)S(1)}, bf16[8,4,64,384]{3,2,1,0:T(8,128)(2,1)S(1)}, bf16[8,4,64,384]{3,2,1,0:T(8,128)(2,1)S(1)}, bf16[8,4,64,384]{3,2,1,0:T(8,128)(2,1)S(1)}) custom-call(bf16[2,4,32,2,64,512]{5,4,3,2,1,0:T(8,128)(2,1)} %u_ref.3, bf16[8,4,4,64,384]{4,3,2,1,0:T(8,128)(2,1)} %bitcast.1.c_ref, ...), custom_call_target="tpu_custom_call" | custom-call | flops 12884901888 | bytes 29360128 | tf_op jit(solution)/shard_map/middle/pallas_call | solution.py:115
  136.6 1.1 copy-done.16
  137.7 1.2 copy-done.18
  138.9 1.1 copy-done.20
  140.0 35.5 %all-to-all-done.2 = bf16[32,4,64,384]{3,2,1,0:T(8,128)(2,1)} async-done(((bf16[32,4,64,384]{3,2,1,0:T(8,128)(2,1)}), bf16[32,4,64,384]{3,2,1,0:T(8,128)(2,1)}, u32[]{:S(2)}, u32[]{:S(2)}) %all-to-all-start.2) | async-done | bytes 6291488 | tf_op jit(solution)/shard_map/all_to_all | solution.py:214
  175.5 3.6 all-to-all-start.8
  179.1 0.0 copy-start.31
  179.1 1.9 copy-done.31
  181.0 30.8 %middle.3 = (bf16[8,4,64,384]{3,2,1,0:T(8,128)(2,1)S(1)}, bf16[8,4,64,384]{3,2,1,0:T(8,128)(2,1)S(1)}, bf16[8,4,64,384]{3,2,1,0:T(8,128)(2,1)S(1)}, bf16[8,4,64,384]{3,2,1,0:T(8,128)(2,1)S(1)}) custom-call(bf16[2,4,32,2,64,512]{5,4,3,2,1,0:T(8,128)(2,1)} %u_ref.3, bf16[8,4,4,64,384]{4,3,2,1,0:T(8,128)(2,1)} %bitcast.4.c_ref, ...), custom_call_target="tpu_custom_call" | custom-call | flops 12884901888 | bytes 29360128 | tf_op jit(solution)/shard_map/middle/pallas_call | solution.py:115
  211.8 0.0 copy-start.15
  211.8 1.1 copy-done.15
  212.9 1.2 copy-done.21
  214.1 1.2 copy-done.23
  215.3 1.2 copy-done.25
  216.5 25.5 %all_to_all.70.rest_1_ = bf16[32,64,384]{2,1,0:T(8,128)(2,1)} all-to-all(bf16[32,64,384]{2,1,0:T(8,128)(2,1)} %bitcast.23), channel_id=1, replica_groups=mesh['freq'=4,'tile'=8] {'tile'}, dimensions={0} | all-to-all | bytes 3145728 | tf_op jit(solution)/shard_map/all_to_all | solution.py:214
  242.0 24.2 %all_to_all.71.rest_0_ = bf16[32,64,384]{2,1,0:T(8,128)(2,1)} all-to-all(bf16[32,64,384]{2,1,0:T(8,128)(2,1)S(1)} %bitcast.19), channel_id=1, replica_groups=mesh['freq'=4,'tile'=8] {'tile'}, dimensions={0} | all-to-all | bytes 3145728 | tf_op jit(solution)/shard_map/all_to_all | solution.py:214
  266.2 24.3 %all_to_all.72.rest_1_ = bf16[32,64,384]{2,1,0:T(8,128)(2,1)} all-to-all(bf16[32,64,384]{2,1,0:T(8,128)(2,1)S(1)} %bitcast.22), channel_id=1, replica_groups=mesh['freq'=4,'tile'=8] {'tile'}, dimensions={0} | all-to-all | bytes 3145728 | tf_op jit(solution)/shard_map/all_to_all | solution.py:214
  290.5 24.2 %all_to_all.73.rest_0_ = bf16[32,64,384]{2,1,0:T(8,128)(2,1)} all-to-all(bf16[32,64,384]{2,1,0:T(8,128)(2,1)S(1)} %bitcast.18), channel_id=1, replica_groups=mesh['freq'=4,'tile'=8] {'tile'}, dimensions={0} | all-to-all | bytes 3145728 | tf_op jit(solution)/shard_map/all_to_all | solution.py:214
  314.8 24.1 %all_to_all.74.rest_1_ = bf16[32,64,384]{2,1,0:T(8,128)(2,1)} all-to-all(bf16[32,64,384]{2,1,0:T(8,128)(2,1)S(1)} %bitcast.21), channel_id=1, replica_groups=mesh['freq'=4,'tile'=8] {'tile'}, dimensions={0} | all-to-all | bytes 3145728 | tf_op jit(solution)/shard_map/all_to_all | solution.py:214
  338.9 23.4 %all_to_all.75.rest_0_ = bf16[32,64,384]{2,1,0:T(8,128)(2,1)S(1)} all-to-all(bf16[32,64,384]{2,1,0:T(8,128)(2,1)S(1)} %bitcast.16), channel_id=1, replica_groups=mesh['freq'=4,'tile'=8] {'tile'}, dimensions={0} | all-to-all | bytes 3145728 | tf_op jit(solution)/shard_map/all_to_all | solution.py:214
  362.3 3.7 all-to-all-start.12
  366.1 1.4 copy-done.7
  367.5 1.4 copy-done.10
  368.9 10.6 %grad.6 = bf16[4,2,192,512]{3,2,1,0:T(8,128)(2,1)S(1)} custom-call(s32[4,32]{1,0:T(4,128)S(1)} %copy-done.29, s32[2,4,32]{2,1,0:T(4,128)S(1)} %copy-done.27, f32[8,2]{1,0:T(8,128)S(1)} %get-tuple-element.22.cos_ref, f32[8,2]{1,0:T(8,128)S(1)} %get-tuple-element.21.sin_ref, bf16[2,4,32,2,64,512]{5,4,3,2,1,0:T(8,128)(2,1)} %v_ref.11, ...), custom_call_target="tpu_custom_call" | custom-call | flops 3221225472 | bytes 11534336 | tf_op jit(solution)/shard_map/grad/pallas_call | solution.py:190
  379.4 1.1 copy-done.13
  380.6 6.3 %all-to-all-done.12.rest_1_ = bf16[32,64,384]{2,1,0:T(8,128)(2,1)S(1)} async-done(((bf16[32,64,384]{2,1,0:T(8,128)(2,1)}), bf16[32,64,384]{2,1,0:T(8,128)(2,1)S(1)}, u32[]{:S(2)}, u32[]{:S(2)}) %all-to-all-start.12) | async-done | bytes 1572896 | tf_op jit(solution)/shard_map/all_to_all | solution.py:214
  386.9 5.7 %all-to-all-start.10 = ((bf16[4,2,192,512]{3,2,1,0:T(8,128)(2,1)}), bf16[4,2,192,512]{3,2,1,0:T(8,128)(2,1)}, u32[]{:S(2)}, u32[]{:S(2)}) async-start(bf16[4,2,192,512]{3,2,1,0:T(8,128)(2,1)} %copy-done.13), calls=%async_computation.10 | async-start | bytes 3145728 | tf_op jit(solution)/shard_map/all_to_all | solution.py:214
  392.6 1.4 copy-done.8
  394.0 1.4 copy-done.9
  395.5 10.6 %grad.5 = bf16[4,2,192,512]{3,2,1,0:T(8,128)(2,1)S(1)} custom-call(s32[4,32]{1,0:T(4,128)S(1)} %copy-done.29, s32[2,4,32]{2,1,0:T(4,128)S(1)} %copy-done.27, f32[8,2]{1,0:T(8,128)S(1)} %get-tuple-element.22.cos_ref, f32[8,2]{1,0:T(8,128)S(1)} %get-tuple-element.21.sin_ref, bf16[2,4,32,2,64,512]{5,4,3,2,1,0:T(8,128)(2,1)} %v_ref.11, ...), custom_call_target="tpu_custom_call" | custom-call | flops 3221225472 | bytes 11534336 | tf_op jit(solution)/shard_map/grad/pallas_call | solution.py:190
  406.0 0.0 copy-start.14
  406.0 1.1 copy-done.14
  407.2 19.7 %all-to-all-done.10 = bf16[4,2,192,512]{3,2,1,0:T(8,128)(2,1)} async-done(((bf16[4,2,192,512]{3,2,1,0:T(8,128)(2,1)}), bf16[4,2,192,512]{3,2,1,0:T(8,128)(2,1)}, u32[]{:S(2)}, u32[]{:S(2)}) %all-to-all-start.10) | async-done | bytes 1572896 | tf_op jit(solution)/shard_map/all_to_all | solution.py:214
  426.8 4.4 all-to-all-start.7
  431.2 1.4 copy-done.4
  432.6 1.4 copy-done.5
  434.1 10.6 %grad.4 = bf16[4,2,192,512]{3,2,1,0:T(8,128)(2,1)S(1)} custom-call(s32[4,32]{1,0:T(4,128)S(1)} %copy-done.29, s32[2,4,32]{2,1,0:T(4,128)S(1)} %copy-done.27, f32[8,2]{1,0:T(8,128)S(1)} %get-tuple-element.22.cos_ref, f32[8,2]{1,0:T(8,128)S(1)} %get-tuple-element.21.sin_ref, bf16[2,4,32,2,64,512]{5,4,3,2,1,0:T(8,128)(2,1)} %v_ref.11, ...), custom_call_target="tpu_custom_call" | custom-call | flops 3221225472 | bytes 11534336 | tf_op jit(solution)/shard_map/grad/pallas_call | solution.py:190
  444.6 1.1 copy-done.12
  445.8 22.0 %all-to-all-done.7 = bf16[4,2,192,512]{3,2,1,0:T(8,128)(2,1)} async-done(((bf16[4,2,192,512]{3,2,1,0:T(8,128)(2,1)}), bf16[4,2,192,512]{3,2,1,0:T(8,128)(2,1)}, u32[]{:S(2)}, u32[]{:S(2)}) %all-to-all-start.7) | async-done | bytes 1572896 | tf_op jit(solution)/shard_map/all_to_all | solution.py:214
  467.8 4.5 all-to-all-start.4
  472.3 10.6 %grad.7 = bf16[4,2,192,512]{3,2,1,0:T(8,128)(2,1)S(1)} custom-call(s32[4,32]{1,0:T(4,128)S(1)} %copy-done.29, s32[2,4,32]{2,1,0:T(4,128)S(1)} %copy-done.27, f32[8,2]{1,0:T(8,128)S(1)} %get-tuple-element.22.cos_ref, f32[8,2]{1,0:T(8,128)S(1)} %get-tuple-element.21.sin_ref, bf16[2,4,32,2,64,512]{5,4,3,2,1,0:T(8,128)(2,1)} %v_ref.11, ...), custom_call_target="tpu_custom_call" | custom-call | flops 3221225472 | bytes 11534336 | tf_op jit(solution)/shard_map/grad/pallas_call | solution.py:190
  482.9 0.0 copy-start.11
  482.9 1.1 copy-done.11
  484.0 24.6 %all-to-all-done.4 = bf16[4,2,192,512]{3,2,1,0:T(8,128)(2,1)} async-done(((bf16[4,2,192,512]{3,2,1,0:T(8,128)(2,1)}), bf16[4,2,192,512]{3,2,1,0:T(8,128)(2,1)}, u32[]{:S(2)}, u32[]{:S(2)}) %all-to-all-start.4) | async-done | bytes 1572896 | tf_op jit(solution)/shard_map/all_to_all | solution.py:214
  508.6 3.6 all-to-all-start.13
  512.2 1.7 convert_reduce_fusion.1
  513.9 1.7 convert_reduce_fusion.2
  515.6 2.6 convert_reduce_fusion.3
  518.2 30.4 %all-to-all-done.13 = bf16[4,2,192,512]{3,2,1,0:T(8,128)(2,1)S(1)} async-done(((bf16[4,2,192,512]{3,2,1,0:T(8,128)(2,1)}), bf16[4,2,192,512]{3,2,1,0:T(8,128)(2,1)S(1)}, u32[]{:S(2)}, u32[]{:S(2)}) %all-to-all-start.13) | async-done | bytes 1572896 | tf_op jit(solution)/shard_map/all_to_all | solution.py:214
  548.6 0.2 convert_reduce_fusion
  548.8 0.9 copy-done.32
  549.7 1.9 maximum_bitcast_fusion
  (40 shorter events, 0.1 us)
Async XLA Ops:
  0.0 1.9 copy-start.2
  1.9 0.7 copy-start.26
  2.6 0.7 copy-start.28
  19.2 2.6 copy-start.1
  21.9 5.4 copy-start.3
  21.9 5.4 copy-start.27
  21.9 5.5 copy-start.29
  21.9 77.3 %all-to-all-start = ((bf16[32,4,64,384]{3,2,1,0:T(8,128)(2,1)}), bf16[32,4,64,384]{3,2,1,0:T(8,128)(2,1)}, u32[]{:S(2)}, u32[]{:S(2)}) async-start(bf16[32,4,64,384]{3,2,1,0:T(8,128)(2,1)} %copy-done.1), calls=%async_computation | async-start | bytes 12582912 | tf_op jit(solution)/shard_map/all_to_all | solution.py:214
  43.3 2.6 copy-start
  99.1 76.3 %all-to-all-start.2 = ((bf16[32,4,64,384]{3,2,1,0:T(8,128)(2,1)}), bf16[32,4,64,384]{3,2,1,0:T(8,128)(2,1)}, u32[]{:S(2)}, u32[]{:S(2)}) async-start(bf16[32,4,64,384]{3,2,1,0:T(8,128)(2,1)} %copy-done), calls=%async_computation.2 | async-start | bytes 12582912 | tf_op jit(solution)/shard_map/all_to_all | solution.py:214
  103.9 1.9 copy-start.30
  136.6 1.1 copy-start.16
  137.7 1.2 copy-start.18
  138.9 1.1 copy-start.20
  175.5 41.0 %all-to-all-start.8 = ((bf16[32,64,384]{2,1,0:T(8,128)(2,1)}), bf16[32,64,384]{2,1,0:T(8,128)(2,1)S(1)}, u32[]{:S(2)}, u32[]{:S(2)}) async-start(bf16[32,64,384]{2,1,0:T(8,128)(2,1)} %bitcast.20), calls=%async_computation.8 | async-start | bytes 3145728 | tf_op jit(solution)/shard_map/all_to_all | solution.py:214
  179.1 1.9 copy-start.31
  211.8 1.1 copy-start.15
  212.9 1.2 copy-start.21
  214.1 1.2 copy-start.23
  215.3 1.2 copy-start.25
  216.5 25.5 %copy-start.6 = (bf16[32,64,384]{2,1,0:T(8,128)(2,1)}, bf16[32,64,384]{2,1,0:T(8,128)(2,1)S(1)}, u32[]{:S(2)}) copy-start(bf16[32,64,384]{2,1,0:T(8,128)(2,1)S(1)} %all-to-all-done.8.rest_0_) | copy-start | bytes 4718596
  216.5 25.5 %copy-start.19 = (bf16[8,4,64,384]{3,2,1,0:T(8,128)(2,1)S(1)}, bf16[8,4,64,384]{3,2,1,0:T(8,128)(2,1)}, u32[]{:S(2)}) copy-start(bf16[8,4,64,384]{3,2,1,0:T(8,128)(2,1)} %copy-done.18) | copy-start | bytes 4718596
  242.0 24.3 %copy-start.24 = (bf16[8,4,64,384]{3,2,1,0:T(8,128)(2,1)S(1)}, bf16[8,4,64,384]{3,2,1,0:T(8,128)(2,1)}, u32[]{:S(2)}) copy-start(bf16[8,4,64,384]{3,2,1,0:T(8,128)(2,1)} %copy-done.23) | copy-start | bytes 4718596
  266.2 24.3 %copy-start.17 = (bf16[8,4,64,384]{3,2,1,0:T(8,128)(2,1)S(1)}, bf16[8,4,64,384]{3,2,1,0:T(8,128)(2,1)}, u32[]{:S(2)}) copy-start(bf16[8,4,64,384]{3,2,1,0:T(8,128)(2,1)} %copy-done.16) | copy-start | bytes 4718596
  290.5 24.2 %copy-start.22 = (bf16[8,4,64,384]{3,2,1,0:T(8,128)(2,1)S(1)}, bf16[8,4,64,384]{3,2,1,0:T(8,128)(2,1)}, u32[]{:S(2)}) copy-start(bf16[8,4,64,384]{3,2,1,0:T(8,128)(2,1)} %copy-done.21) | copy-start | bytes 4718596
  362.3 3.7 copy-start.33
  362.3 24.7 %all-to-all-start.12 = ((bf16[32,64,384]{2,1,0:T(8,128)(2,1)}), bf16[32,64,384]{2,1,0:T(8,128)(2,1)S(1)}, u32[]{:S(2)}, u32[]{:S(2)}) async-start(bf16[32,64,384]{2,1,0:T(8,128)(2,1)} %bitcast.17), calls=%async_computation.12 | async-start | bytes 3145728 | tf_op jit(solution)/shard_map/all_to_all | solution.py:214
  366.0 1.4 copy-start.7
  367.5 1.4 copy-start.10
  379.4 1.2 copy-start.13
  386.9 39.9 %all-to-all-start.10 = ((bf16[4,2,192,512]{3,2,1,0:T(8,128)(2,1)}), bf16[4,2,192,512]{3,2,1,0:T(8,128)(2,1)}, u32[]{:S(2)}, u32[]{:S(2)}) async-start(bf16[4,2,192,512]{3,2,1,0:T(8,128)(2,1)} %copy-done.13), calls=%async_computation.10 | async-start | bytes 3145728 | tf_op jit(solution)/shard_map/all_to_all | solution.py:214
  392.6 1.4 copy-start.8
  394.0 1.4 copy-start.9
  406.0 1.1 copy-start.14
  426.8 40.9 %all-to-all-start.7 = ((bf16[4,2,192,512]{3,2,1,0:T(8,128)(2,1)}), bf16[4,2,192,512]{3,2,1,0:T(8,128)(2,1)}, u32[]{:S(2)}, u32[]{:S(2)}) async-start(bf16[4,2,192,512]{3,2,1,0:T(8,128)(2,1)} %copy-done.14), calls=%async_computation.7 | async-start | bytes 3145728 | tf_op jit(solution)/shard_map/all_to_all | solution.py:214
  431.2 1.4 copy-start.4
  432.6 1.4 copy-start.5
  444.6 1.1 copy-start.12
  467.8 40.9 %all-to-all-start.4 = ((bf16[4,2,192,512]{3,2,1,0:T(8,128)(2,1)}), bf16[4,2,192,512]{3,2,1,0:T(8,128)(2,1)}, u32[]{:S(2)}, u32[]{:S(2)}) async-start(bf16[4,2,192,512]{3,2,1,0:T(8,128)(2,1)} %copy-done.12), calls=%async_computation.4 | async-start | bytes 3145728 | tf_op jit(solution)/shard_map/all_to_all | solution.py:214
  482.9 1.1 copy-start.11
  508.6 40.0 %all-to-all-start.13 = ((bf16[4,2,192,512]{3,2,1,0:T(8,128)(2,1)}), bf16[4,2,192,512]{3,2,1,0:T(8,128)(2,1)S(1)}, u32[]{:S(2)}, u32[]{:S(2)}) async-start(bf16[4,2,192,512]{3,2,1,0:T(8,128)(2,1)} %copy-done.11), calls=%async_computation.13 | async-start | bytes 3145728 | tf_op jit(solution)/shard_map/all_to_all | solution.py:214
  548.6 1.1 copy-start.32

commit v2 on v1

--- a/solution.py
+++ b/solution.py
@@ -79,6 +79,10 @@
     )(tile_rows, tile_rank, v_factor, blocks)
 
 
+def cuts_of(own):
+    return 2 if own % 2 == 0 else 1
+
+
 def middle_body(u_ref, c_ref, seen_ref, *rest):
     outs, (acc_ref, resid_ref, resid2_ref) = rest[:-3], rest[-3:]
     sources, own, rank, cols = c_ref.shape[0], c_ref.shape[2], c_ref.shape[3], c_ref.shape[4]
@@ -103,15 +107,18 @@
         total = dot(part_of(u_ref, (0, 0), first * own, per * own, 0), resid_ref[...])
         total += dot(part_of(u_ref, (0, 0), first * own, per * own, 1), resid2_ref[...])
         back = total.astype(jnp.bfloat16).reshape(per, own, rank, cols)
+        each = own // len(outs)
         for d in range(per):
             for j in range(own):
-                outs[j][first + d, 0] = back[d, j]
+                outs[j // each][first + d, 0, j % each] = back[d, j]
 
 
 def middle_call(freq, u_factor, arrived, seen):
     _, own, tiles, _, rank, width = u_factor.shape
     sources = tiles // own
     cols = seen.shape[-1]
+    cuts = cuts_of(own)
+    each = own // cuts
     return pl.pallas_call(
         middle_body,
         grid=(own,),
@@ -120,8 +127,8 @@
             pl.BlockSpec((sources, 1, own, rank, cols), lambda i: (0, i, 0, 0, 0)),
             pl.BlockSpec((1, 1, width, cols), lambda i: (freq, i, 0, 0)),
         ],
-        out_specs=[pl.BlockSpec((sources, 1, rank, cols), lambda i: (0, i, 0, 0))] * own,
-        out_shape=[jax.ShapeDtypeStruct((sources, own, rank, cols), jnp.bfloat16)] * own,
+        out_specs=[pl.BlockSpec((sources, 1, each, rank, cols), lambda i: (0, i, 0, 0, 0))] * cuts,
+        out_shape=[jax.ShapeDtypeStruct((sources, own, each, rank, cols), jnp.bfloat16)] * cuts,
         scratch_shapes=[
             pltpu.VMEM((width, cols), jnp.float32),
             pltpu.VMEM((width, cols), jnp.bfloat16),
@@ -137,8 +144,8 @@
     )(u_factor, arrived.reshape(sources, own, own, rank, cols), seen)
 
 
-def grad_body(block, freqs, rows_ref, rank_ref, cos_ref, sin_ref, v_ref, *rest):
-    backs, out_ref, acc_ref = rest[:freqs], rest[freqs], rest[freqs + 1]
+def grad_body(block, freqs, groups, rows_ref, rank_ref, cos_ref, sin_ref, v_ref, *rest):
+    backs, outs, acc_ref = rest[:freqs], rest[-1 - groups : -1], rest[-1]
     freq = pl.program_id(0)
     tiles, rank = v_ref.shape[2], v_ref.shape[4]
     cols = acc_ref.shape[1]
@@ -158,7 +165,7 @@
                 for t in range(group):
                     slot = first + t
                     kept = row < rank_ref[f, block, slot]
-                    tile = backs[f][rows_ref[block, slot]]
+                    tile = backs[f][rows_ref[block, slot], 0]
                     picked.append(jnp.where(kept, tile, jnp.zeros_like(tile)))
                 back = jnp.concatenate(picked, 0)
                 acc_ref[f] += dot_rows(back, part_of(v_ref, (0, 0), first, group, 0)) + dot_rows(
@@ -168,7 +175,7 @@
     @pl.when(freq == freqs - 1)
     def _():
         chunk = 16
-        pairs = out_ref.shape[1]
+        pairs = outs[0].shape[0]
 
         @pl.loop(0, half // chunk)
         def _(step):
@@ -179,27 +186,37 @@
                 total = real[0] * cos_ref[lag, 0] - imag[0] * sin_ref[lag, 0]
                 for f in range(1, freqs):
                     total += real[f] * cos_ref[lag, f] - imag[f] * sin_ref[lag, f]
-                out_ref[lag // pairs, lag % pairs, here] = total.astype(out_ref.dtype)
-
-
-def grad_call(block, tile_rows, tile_rank, cosine, sine, v_factor, backs, groups):
+                outs[lag // pairs][lag % pairs, here] = total.astype(jnp.bfloat16)
+
+
+def grad_call(block, tile_rows, tile_rank, cosine, sine, v_factor, backs, groups, held):
     freqs, own, tiles, _, rank, width = v_factor.shape
     cols = backs[0].shape[-1]
     lags = cosine.shape[0]
-    whole = pl.BlockSpec((tiles, rank, cols), lambda f, *_: (0, 0, 0))
+    each = backs[0].shape[1]
+    whole = pl.BlockSpec((tiles, 1, rank, cols), lambda f, *_: (0, block % each, 0, 0))
+    share = (lags // groups, cols // 2, width)
     return pl.pallas_call(
-        functools.partial(grad_body, block, freqs),
+        functools.partial(grad_body, block, freqs, groups),
         grid_spec=pltpu.PrefetchScalarGridSpec(
             num_scalar_prefetch=4,
             grid=(freqs,),
             in_specs=[
                 pl.BlockSpec((1, 1, tiles, 2, rank, width), lambda f, *_: (f, block, 0, 0, 0, 0)),
                 *[whole] * freqs,
+                *[pl.BlockSpec(memory_space=pl.ANY)] * len(held),
             ],
-            out_specs=pl.BlockSpec((groups, lags // groups, cols // 2, width), lambda f, *_: (0, 0, 0, 0)),
+            out_specs=[
+                *[pl.BlockSpec(memory_space=pl.ANY)] * len(held),
+                *[pl.BlockSpec(share, lambda f, *_: (0, 0, 0))] * groups,
+            ],
             scratch_shapes=[pltpu.VMEM((freqs, cols, width), jnp.float32)],
         ),
-        out_shape=jax.ShapeDtypeStruct((groups, lags // groups, cols // 2, width), jnp.bfloat16),
+        out_shape=[
+            *[jax.ShapeDtypeStruct(one.shape, one.dtype) for one in held],
+            *[jax.ShapeDtypeStruct(share, jnp.bfloat16)] * groups,
+        ],
+        input_output_aliases={5 + freqs + n: n for n in range(len(held))},
         compiler_params=pltpu.CompilerParams(vmem_limit_bytes=VMEM_BYTES),
         cost_estimate=pl.CostEstimate(
             flops=4 * freqs * tiles * rank * width * cols,
@@ -207,7 +224,7 @@
             transcendentals=0,
         ),
         name="grad",
-    )(tile_rows, tile_rank, cosine, sine, v_factor, *backs)
+    )(tile_rows, tile_rank, cosine, sine, v_factor, *backs, *held)
 
 
 def exchange(array, axis):
@@ -221,21 +238,33 @@
     blocks = model_freq.reshape(freqs, own, width, cols)
     seen = recorded.reshape(freqs, own, width, cols)
     total = freqs * groups
-    phase = jnp.arange(total, dtype=jnp.float32)[:, None] * omega[None, :]
+    group = lax.axis_index("freq")
+    lag = (jnp.arange(total, dtype=jnp.int32) + group * (total // groups)) % total
+    phase = lag.astype(jnp.float32)[:, None] * omega[None, :]
     cosine = jnp.cos(phase) * (2.0 / total)
     sine = jnp.sin(phase) * (2.0 / total)
 
     arrived = []
     for f in range(freqs):
         arrived.append(exchange(coeff_call(f, tile_rows, tile_rank, v_factor, blocks), "tile"))
-    backs = [middle_call(f, u_factor, arrived[f], seen) for f in range(freqs)]
+    backs = [list(middle_call(f, u_factor, arrived[f], seen)) for f in range(freqs)]
     parts = []
-    for j in range(own):
+    each = own // cuts_of(own)
+    for cut in range(cuts_of(own)):
         returned = [
-            exchange(backs[f][j].reshape(tiles, rank, cols), "tile").reshape(tiles, rank, cols) for f in range(freqs)
+            exchange(backs[f][cut].reshape(tiles, each, rank, cols), "tile") for f in range(freqs)
         ]
-        shares = grad_call(j, tile_rows, tile_rank, cosine, sine, v_factor, returned, groups)
-        parts.append(jnp.sum(exchange(shares, "freq").astype(jnp.float32), 0))
+        for j in range(cut * each, (cut + 1) * each):
+            held = [backs[-1][cut + 1]] if cut + 1 < cuts_of(own) else []
+            shares = grad_call(j, tile_rows, tile_rank, cosine, sine, v_factor, returned, groups, held)
+            if held:
+                backs[-1][cut + 1] = shares[0]
+                shares = shares[1:]
+            summed = shares[0].astype(jnp.float32)
+            for d in range(1, groups):
+                step = [(z, (z + d) % groups) for z in range(groups)]
+                summed += lax.ppermute(shares[d], "freq", step).astype(jnp.float32)
+            parts.append(summed)
     return jnp.swapaxes(jnp.concatenate(parts, 2), 1, 2)
 
 

time: 554 us -> 447 us (0.81)
  blocking collectives: 146 us -> 42.3 us
  waiting for transfers between devices: 192 us -> 152 us
  starting transfers between devices: 35.6 us -> 73.7 us
  local copies, waits for them, and re-layouts: 34.3 us -> 28 us
    all_to_all x6 -> x1, blocking collectives: 146 us -> 42.3 us  [exchange(): return lax.all_to_all(array, axis, split_axis=0, concat_axis=0, tiled=True)]
    all_to_all x8 -> x5, waiting for transfers between devices: 192 us -> 127 us  [exchange(): return lax.all_to_all(array, axis, split_axis=0, concat_axis=0, tiled=True)]
    ppermute x0 -> x12, starting transfers between devices: none -> 51.6 us  [per_device(): summed += lax.ppermute(shares[d], 'freq', step).astype(jnp.float32)]
    ppermute x0 -> x12, waiting for transfers between devices: none -> 24.9 us  [per_device(): summed += lax.ppermute(shares[d], 'freq', step).astype(jnp.float32)]
    all_to_all x8 -> x5, starting transfers between devices: 35.6 us -> 22.1 us  [exchange(): return lax.all_to_all(array, axis, split_axis=0, concat_axis=0, tiled=True)]
    unnamed x68 -> x56, local copies, waits for them, and re-layouts: 34.3 us -> 28 us
    reduce_sum x4 -> x0, other arithmetic: 6.27 us -> none  [per_device(): parts.append(jnp.sum(exchange(shares, 'freq').astype(jnp.float32), 0))]
  transfers between devices with their start and end apart: 8 -> 17, of which waited for: 7 -> 7; matrix products, arithmetic and copies ran while one was open for 1% -> 1% of each run, Pallas kernels for 22% -> 28%
where the time goes in v2:
time: 447 us; the launch traced here: 440 us
  waiting for transfers between devices  152 us (34%)
  Pallas kernels  138 us (31%)
  starting transfers between devices  73.7 us (16%)
  blocking collectives  42.3 us (9%)
  local copies, waits for them, and re-layouts  28 us (6%)
  other arithmetic  5.17 us (1%)
    all_to_all x5, waiting for transfers between devices, exchange(): return lax.all_to_all(array, axis, split_axis=0, concat_axis=0, tiled=True)  127 us
    pallas_call x2, Pallas kernels, middle_call(): pl.pallas_call(middle_body, grid=(own,), in_specs=[pl.BlockSpec((1, 1, ti...  61.6 us
    ppermute x12, starting transfers between devices, per_device(): summed += lax.ppermute(shares[d], 'freq', step).astype(jnp.float32)  51.6 us
    pallas_call x4, Pallas kernels, grad_call(): pl.pallas_call(functools.partial(grad_body, block, freqs, groups), grid_s...  44.5 us
    all_to_all x1, blocking collectives, exchange(): return lax.all_to_all(array, axis, split_axis=0, concat_axis=0, tiled=True)  42.3 us
    pallas_call x2, Pallas kernels, coeff_call(): pl.pallas_call(functools.partial(coeff_body, freq), grid_spec=pltpu.Prefe...  31.9 us
    unnamed x56, local copies, waits for them, and re-layouts  28 us
    ppermute x12, waiting for transfers between devices, per_device(): summed += lax.ppermute(shares[d], 'freq', step).astype(jnp.float32)  24.9 us
  transfers between devices with their start and end apart: 17, of which 7 were waited for; matrix products, arithmetic and copies ran while one was open for 1% of the time, Pallas kernels for 28%

profile of v2, /device:TPU:0, one launch (start us, length us, event | category | flops | bytes accessed | tf_op | source)
XLA Modules:
  0.0 439.8 jit_solution(3459659321263470058)
XLA Ops:
  0.0 1.9 copy-done.7
  1.9 0.7 copy-done.14
  2.6 0.7 copy-done.16
  3.3 16.0 %coeff.2 = bf16[32,4,64,384]{3,2,1,0:T(8,128)(2,1)S(1)} custom-call(s32[4,32]{1,0:T(4,128)S(1)} %copy-done.16, s32[2,4,32]{2,1,0:T(4,128)S(1)} %copy-done.14, bf16[2,4,32,2,64,512]{5,4,3,2,1,0:T(8,128)(2,1)} %v_ref.11, bf16[2,4,512,384]{3,2,1,0:T(8,128)(2,1)S(1)} %bitcast.11), custom_call_target="tpu_custom_call" | custom-call | flops 6442450944 | bytes 23068672 | tf_op jit(solution)/shard_map/coeff/pallas_call | solution.py:59
  19.2 2.6 copy-done.6
  21.8 5.4 %all-to-all-start = ((bf16[32,4,64,384]{3,2,1,0:T(8,128)(2,1)}), bf16[32,4,64,384]{3,2,1,0:T(8,128)(2,1)}, u32[]{:S(2)}, u32[]{:S(2)}) async-start(bf16[32,4,64,384]{3,2,1,0:T(8,128)(2,1)} %copy-done.6), calls=%async_computation | async-start | bytes 12582912 | tf_op jit(solution)/shard_map/all_to_all | solution.py:231
  27.3 16.0 %coeff.3 = bf16[32,4,64,384]{3,2,1,0:T(8,128)(2,1)S(1)} custom-call(s32[4,32]{1,0:T(4,128)S(1)} %copy-done.17, s32[2,4,32]{2,1,0:T(4,128)S(1)} %copy-done.15, bf16[2,4,32,2,64,512]{5,4,3,2,1,0:T(8,128)(2,1)} %v_ref.11, bf16[2,4,512,384]{3,2,1,0:T(8,128)(2,1)S(1)} %bitcast.12), custom_call_target="tpu_custom_call" | custom-call | flops 6442450944 | bytes 23068672 | tf_op jit(solution)/shard_map/coeff/pallas_call | solution.py:59
  43.3 2.7 copy-done.5
  46.0 53.2 %all-to-all-done = bf16[32,4,64,384]{3,2,1,0:T(8,128)(2,1)} async-done(((bf16[32,4,64,384]{3,2,1,0:T(8,128)(2,1)}), bf16[32,4,64,384]{3,2,1,0:T(8,128)(2,1)}, u32[]{:S(2)}, u32[]{:S(2)}) %all-to-all-start) | async-done | bytes 6291488 | tf_op jit(solution)/shard_map/all_to_all | solution.py:231
  99.2 4.7 %all-to-all-start.2 = ((bf16[32,4,64,384]{3,2,1,0:T(8,128)(2,1)}), bf16[32,4,64,384]{3,2,1,0:T(8,128)(2,1)}, u32[]{:S(2)}, u32[]{:S(2)}) async-start(bf16[32,4,64,384]{3,2,1,0:T(8,128)(2,1)} %copy-done.5), calls=%async_computation.2 | async-start | bytes 12582912 | tf_op jit(solution)/shard_map/all_to_all | solution.py:231
  103.9 30.8 %middle.2 = (bf16[8,4,2,64,384]{4,3,2,1,0:T(8,128)(2,1)S(1)}, bf16[8,4,2,64,384]{4,3,2,1,0:T(8,128)(2,1)S(1)}) custom-call(bf16[2,4,32,2,64,512]{5,4,3,2,1,0:T(8,128)(2,1)} %u_ref.3, bf16[8,4,4,64,384]{4,3,2,1,0:T(8,128)(2,1)} %bitcast.1.c_ref, bf16[2,4,512,384]{3,2,1,0:T(8,128)(2,1)S(1)} %bitcast.16), custom_call_target="tpu_custom_call" | custom-call | flops 12884901888 | bytes 29360128 | tf_op jit(solution)/shard_map/middle/pallas_call | solution.py:122
  134.7 0.0 copy-start.9
  134.7 1.7 copy-done.9
  136.4 1.7 copy-done.10
  138.1 37.4 %all-to-all-done.2 = bf16[32,4,64,384]{3,2,1,0:T(8,128)(2,1)} async-done(((bf16[32,4,64,384]{3,2,1,0:T(8,128)(2,1)}), bf16[32,4,64,384]{3,2,1,0:T(8,128)(2,1)}, u32[]{:S(2)}, u32[]{:S(2)}) %all-to-all-start.2) | async-done | bytes 6291488 | tf_op jit(solution)/shard_map/all_to_all | solution.py:231
  175.5 3.6 all-to-all-start.1
  179.2 0.0 copy-start.19
  179.2 1.9 copy-done.19
  181.1 30.8 %middle.3 = (bf16[8,4,2,64,384]{4,3,2,1,0:T(8,128)(2,1)S(1)}, bf16[8,4,2,64,384]{4,3,2,1,0:T(8,128)(2,1)S(1)}) custom-call(bf16[2,4,32,2,64,512]{5,4,3,2,1,0:T(8,128)(2,1)} %u_ref.3, bf16[8,4,4,64,384]{4,3,2,1,0:T(8,128)(2,1)} %bitcast.4.c_ref, bf16[2,4,512,384]{3,2,1,0:T(8,128)(2,1)S(1)} %bitcast.17), custom_call_target="tpu_custom_call" | custom-call | flops 12884901888 | bytes 29360128 | tf_op jit(solution)/shard_map/middle/pallas_call | solution.py:122
  211.9 1.7 copy-done.2
  213.5 1.7 copy-done.11
  215.3 1.7 all-to-all-done.1.rest_0_
  217.0 42.3 %all_to_all.30.rest_1_ = bf16[32,2,64,384]{3,2,1,0:T(8,128)(2,1)} all-to-all(bf16[32,2,64,384]{3,2,1,0:T(8,128)(2,1)} %bitcast.15), channel_id=1, replica_groups=mesh['freq'=4,'tile'=8] {'tile'}, dimensions={0} | all-to-all | bytes 6291456 | tf_op jit(solution)/shard_map/all_to_all | solution.py:231
  259.3 3.8 all-to-all-start.4
  263.1 0.1 fusion.1
  263.2 1.9 copy-done.1
  265.1 1.9 copy-done.3
  267.0 11.1 %grad.4 = (bf16[8,4,2,64,384]{4,3,2,1,0:T(8,128)(2,1)S(1)}, bf16[2,192,512]{2,1,0:T(8,128)(2,1)S(1)}, bf16[2,192,512]{2,1,0:T(8,128)(2,1)S(1)}, bf16[2,192,512]{2,1,0:T(8,128)(2,1)S(1)}, bf16[2,192,512]{2,1,0:T(8,128)(2,1)S(1)}) custom-call(s32[4,32]{1,0:T(4,128)S(1)} %copy-done.17, s32[2,4,32]{2,1,0:T(4,128)S(1)} %copy-done.15, ...), custom_call_target="tpu_custom_call", output_to_operand_aliasing={{0}: (7, {})} | custom-call | flops 3221225472 | bytes 11534336 | tf_op jit(solution)/shard_map/grad/pallas_call | solution.py:199
  278.1 0.8 copy-done.20
  278.9 0.7 copy-done.22
  279.6 0.7 copy-done.23
  280.4 11.1 %grad.5 = (bf16[8,4,2,64,384]{4,3,2,1,0:T(8,128)(2,1)S(1)}, bf16[2,192,512]{2,1,0:T(8,128)(2,1)S(1)}, bf16[2,192,512]{2,1,0:T(8,128)(2,1)S(1)}, bf16[2,192,512]{2,1,0:T(8,128)(2,1)S(1)}, bf16[2,192,512]{2,1,0:T(8,128)(2,1)S(1)}) custom-call(s32[4,32]{1,0:T(4,128)S(1)} %copy-done.17, s32[2,4,32]{2,1,0:T(4,128)S(1)} %copy-done.15, ...), custom_call_target="tpu_custom_call", output_to_operand_aliasing={{0}: (7, {})} | custom-call | flops 3221225472 | bytes 11534336 | tf_op jit(solution)/shard_map/grad/pallas_call | solution.py:199
  291.5 1.7 copy-done.4
  293.2 0.8 copy-done.12
  294.0 0.7 copy-done.24
  294.7 0.8 copy-done.25
  295.5 0.8 copy-done.26
  296.3 4.6 %all-to-all-done.4.rest_0_ = bf16[32,2,64,384]{3,2,1,0:T(8,128)(2,1)S(1)} async-done(((bf16[32,2,64,384]{3,2,1,0:T(8,128)(2,1)}), bf16[32,2,64,384]{3,2,1,0:T(8,128)(2,1)S(1)}, u32[]{:S(2)}, u32[]{:S(2)}) %all-to-all-start.4) | async-done | bytes 3145760 | tf_op jit(solution)/shard_map/all_to_all | solution.py:231
  300.9 4.5 %all-to-all-start.5 = ((bf16[32,2,64,384]{3,2,1,0:T(8,128)(2,1)}), bf16[32,2,64,384]{3,2,1,0:T(8,128)(2,1)}, u32[]{:S(2)}, u32[]{:S(2)}) async-start(bf16[32,2,64,384]{3,2,1,0:T(8,128)(2,1)} %bitcast.10), calls=%async_computation.5 | async-start | bytes 6291456 | tf_op jit(solution)/shard_map/all_to_all | solution.py:231
  305.3 2.4 collective-permute-start.3
  307.7 2.6 collective-permute-start.4
  310.3 1.3 collective-permute-start.5
  311.6 0.7 collective-permute-start
  312.3 0.3 collective-permute-start.1
  312.7 30.6 %all-to-all-done.5.rest_1_ = bf16[32,2,64,384]{3,2,1,0:T(8,128)(2,1)} async-done(((bf16[32,2,64,384]{3,2,1,0:T(8,128)(2,1)}), bf16[32,2,64,384]{3,2,1,0:T(8,128)(2,1)}, u32[]{:S(2)}, u32[]{:S(2)}) %all-to-all-start.5) | async-done | bytes 3145760 | tf_op jit(solution)/shard_map/all_to_all | solution.py:231
  343.2 11.1 %grad.6 = (bf16[2,192,512]{2,1,0:T(8,128)(2,1)S(1)}, bf16[2,192,512]{2,1,0:T(8,128)(2,1)S(1)}, bf16[2,192,512]{2,1,0:T(8,128)(2,1)S(1)}, bf16[2,192,512]{2,1,0:T(8,128)(2,1)S(1)}) custom-call(s32[4,32]{1,0:T(4,128)S(1)} %copy-done.17, s32[2,4,32]{2,1,0:T(4,128)S(1)} %copy-done.15, f32[8,2]{1,0:T(8,128)S(1)} %get-tuple-element.50.cos_ref, ...), custom_call_target="tpu_custom_call" | custom-call | flops 3221225472 | bytes 11534336 | tf_op jit(solution)/shard_map/grad/pallas_call | solution.py:199
  354.4 0.0 collective-permute-done.3
  354.4 4.4 %collective-permute-start.2 = (bf16[2,192,512]{2,1,0:T(8,128)(2,1)S(1)}, bf16[2,192,512]{2,1,0:T(8,128)(2,1)S(1)}, u32[]{:S(2)}, u32[]{:S(2)}) collective-permute-start(bf16[2,192,512]{2,1,0:T(8,128)(2,1)S(1)} %copy-done.21), channel_id=1, source_target_pairs={{0,24},{8,0},{16,8},{24,16},{1,25},{9,1},{17,9},{25,17},{2,26},{10... | collective-permute-start | bytes 1179656 | tf_op jit(solution)/shard_map/ppermute | solution.py:266
  358.8 0.0 collective-permute-done.5
  358.8 1.4 convert_add_fusion.2
  360.3 3.3 collective-permute-start.7
  363.5 3.7 collective-permute-start.8
  367.2 11.1 %grad.7 = (bf16[2,192,512]{2,1,0:T(8,128)(2,1)S(1)}, bf16[2,192,512]{2,1,0:T(8,128)(2,1)S(1)}, bf16[2,192,512]{2,1,0:T(8,128)(2,1)S(1)}, bf16[2,192,512]{2,1,0:T(8,128)(2,1)S(1)}) custom-call(s32[4,32]{1,0:T(4,128)S(1)} %copy-done.17, s32[2,4,32]{2,1,0:T(4,128)S(1)} %copy-done.15, f32[8,2]{1,0:T(8,128)S(1)} %get-tuple-element.50.cos_ref, ...), custom_call_target="tpu_custom_call" | custom-call | flops 3221225472 | bytes 11534336 | tf_op jit(solution)/shard_map/grad/pallas_call | solution.py:199
  378.3 8.8 %collective-permute-done.1 = bf16[2,192,512]{2,1,0:T(8,128)(2,1)} collective-permute-done((bf16[2,192,512]{2,1,0:T(8,128)(2,1)}, bf16[2,192,512]{2,1,0:T(8,128)(2,1)}, u32[]{:S(2)}, u32[]{:S(2)}) %collective-permute-start.1) | collective-permute-done | bytes 393248 | tf_op jit(solution)/shard_map/ppermute | solution.py:266
  387.2 0.0 collective-permute-done.2
  387.2 19.0 %collective-permute-start.11 = (bf16[2,192,512]{2,1,0:T(8,128)(2,1)S(1)}, bf16[2,192,512]{2,1,0:T(8,128)(2,1)S(1)}, u32[]{:S(2)}, u32[]{:S(2)}) collective-permute-start(bf16[2,192,512]{2,1,0:T(8,128)(2,1)S(1)} %get-tuple-element.48), channel_id=1, source_target_pairs={{0,24},{8,0},{16,8},{24,16},{1,25},{9,1},{17,9},{25,17},{2,26},{10... | collective-permute-start | bytes 1179656 | tf_op jit(solution)/shard_map/ppermute | solution.py:266
  406.2 13.9 %collective-permute-start.9 = (bf16[2,192,512]{2,1,0:T(8,128)(2,1)S(1)}, bf16[2,192,512]{2,1,0:T(8,128)(2,1)S(1)}, u32[]{:S(2)}, u32[]{:S(2)}) collective-permute-start(bf16[2,192,512]{2,1,0:T(8,128)(2,1)S(1)} %get-tuple-element.46), channel_id=1, source_target_pairs={{0,8},{8,16},{16,24},{24,0},{1,9},{9,17},{17,25},{25,1},{2,10},{10... | collective-permute-start | bytes 1179656 | tf_op jit(solution)/shard_map/ppermute | solution.py:266
  420.1 1.3 convert_add_fusion.3
  421.4 0.0 collective-permute-done.8
  421.4 0.2 convert_add_fusion.1
  421.6 16.0 %collective-permute-done.10 = bf16[2,192,512]{2,1,0:T(8,128)(2,1)S(1)} collective-permute-done((bf16[2,192,512]{2,1,0:T(8,128)(2,1)S(1)}, bf16[2,192,512]{2,1,0:T(8,128)(2,1)S(1)}, u32[]{:S(2)}, u32[]{:S(2)}) %collective-permute-start.10) | collective-permute-done | bytes 393248 | tf_op jit(solution)/shard_map/ppermute | solution.py:266
  437.6 0.0 collective-permute-done.11
  437.6 0.2 convert_add_fusion
  437.8 1.9 maximum_bitcast_fusion
  (42 shorter events, 0.1 us)
Async XLA Ops:
  0.0 1.9 copy-start.7
  1.9 0.7 copy-start.14
  2.6 0.7 copy-start.16
  19.2 2.6 copy-start.6
  21.8 5.4 %copy-start.8 = (bf16[2,2048,384]{2,1,0:T(8,128)(2,1)S(1)}, bf16[2,2048,384]{2,1,0:T(8,128)(2,1)}, u32[]{:S(2)}) copy-start(bf16[2,2048,384]{2,1,0:T(8,128)(2,1)} %param.7) | copy-start | bytes 9437188
  21.8 5.4 %copy-start.15 = (s32[2,4,32]{2,1,0:T(4,128)S(1)}, s32[2,4,32]{2,1,0:T(4,128)}, u32[]{:S(2)}) copy-start(s32[2,4,32]{2,1,0:T(4,128)} %rank_ref.11) | copy-start | bytes 3076
  21.8 5.5 %copy-start.17 = (s32[4,32]{1,0:T(4,128)S(1)}, s32[4,32]{1,0:T(4,128)}, u32[]{:S(2)}) copy-start(s32[4,32]{1,0:T(4,128)} %rows_ref.11) | copy-start | bytes 1540
  21.8 77.3 %all-to-all-start = ((bf16[32,4,64,384]{3,2,1,0:T(8,128)(2,1)}), bf16[32,4,64,384]{3,2,1,0:T(8,128)(2,1)}, u32[]{:S(2)}, u32[]{:S(2)}) async-start(bf16[32,4,64,384]{3,2,1,0:T(8,128)(2,1)} %copy-done.6), calls=%async_computation | async-start | bytes 12582912 | tf_op jit(solution)/shard_map/all_to_all | solution.py:231
  43.3 2.7 copy-start.5
  46.0 58.0 %copy-start.18 = (bf16[2,2048,384]{2,1,0:T(8,128)(2,1)S(1)}, bf16[2,2048,384]{2,1,0:T(8,128)(2,1)}, u32[]{:S(2)}) copy-start(bf16[2,2048,384]{2,1,0:T(8,128)(2,1)} %param.8) | copy-start | bytes 9437188
  99.2 76.4 %all-to-all-start.2 = ((bf16[32,4,64,384]{3,2,1,0:T(8,128)(2,1)}), bf16[32,4,64,384]{3,2,1,0:T(8,128)(2,1)}, u32[]{:S(2)}, u32[]{:S(2)}) async-start(bf16[32,4,64,384]{3,2,1,0:T(8,128)(2,1)} %copy-done.5), calls=%async_computation.2 | async-start | bytes 12582912 | tf_op jit(solution)/shard_map/all_to_all | solution.py:231
  134.7 1.7 copy-start.9
  136.4 1.7 copy-start.10
  175.5 41.5 %all-to-all-start.1 = ((bf16[32,2,64,384]{3,2,1,0:T(8,128)(2,1)}), bf16[32,2,64,384]{3,2,1,0:T(8,128)(2,1)S(1)}, u32[]{:S(2)}, u32[]{:S(2)}) async-start(bf16[32,2,64,384]{3,2,1,0:T(8,128)(2,1)} %bitcast.14), calls=%async_computation.1 | async-start | bytes 6291456 | tf_op jit(solution)/shard_map/all_to_all | solution.py:231
  179.2 1.9 copy-start.19
  211.9 1.7 copy-start.2
  213.5 1.7 copy-start.11
  217.0 42.3 %copy-start = (bf16[32,2,64,384]{3,2,1,0:T(8,128)(2,1)}, bf16[32,2,64,384]{3,2,1,0:T(8,128)(2,1)S(1)}, u32[]{:S(2)}) copy-start(bf16[32,2,64,384]{3,2,1,0:T(8,128)(2,1)S(1)} %all-to-all-done.1.rest_0_) | copy-start | bytes 9437188
  259.3 3.8 copy-start.27
  259.3 41.6 %all-to-all-start.4 = ((bf16[32,2,64,384]{3,2,1,0:T(8,128)(2,1)}), bf16[32,2,64,384]{3,2,1,0:T(8,128)(2,1)S(1)}, u32[]{:S(2)}, u32[]{:S(2)}) async-start(bf16[32,2,64,384]{3,2,1,0:T(8,128)(2,1)} %bitcast.13), calls=%async_computation.4 | async-start | bytes 6291456 | tf_op jit(solution)/shard_map/all_to_all | solution.py:231
  263.2 1.9 copy-start.1
  265.1 1.9 copy-start.3
  278.1 0.8 copy-start.20
  278.9 0.7 copy-start.22
  279.6 0.7 copy-start.23
  291.5 1.7 copy-start.4
  293.2 0.8 copy-start.12
  294.0 0.8 copy-start.24
  294.7 0.8 copy-start.25
  295.5 0.8 copy-start.26
  300.9 42.4 %all-to-all-start.5 = ((bf16[32,2,64,384]{3,2,1,0:T(8,128)(2,1)}), bf16[32,2,64,384]{3,2,1,0:T(8,128)(2,1)}, u32[]{:S(2)}, u32[]{:S(2)}) async-start(bf16[32,2,64,384]{3,2,1,0:T(8,128)(2,1)} %bitcast.10), calls=%async_computation.5 | async-start | bytes 6291456 | tf_op jit(solution)/shard_map/all_to_all | solution.py:231
  305.3 49.0 %collective-permute-start.3 = (bf16[2,192,512]{2,1,0:T(8,128)(2,1)}, bf16[2,192,512]{2,1,0:T(8,128)(2,1)}, u32[]{:S(2)}, u32[]{:S(2)}) collective-permute-start(bf16[2,192,512]{2,1,0:T(8,128)(2,1)} %copy-done.26), channel_id=1, source_target_pairs={{0,8},{8,16},{16,24},{24,0},{1,9},{9,17},{17,25},{25,1},{2,10},{10... | collective-permute-start | bytes 1179656 | tf_op jit(solution)/shard_map/ppermute | solution.py:266
  307.7 51.1 %collective-permute-start.4 = (bf16[2,192,512]{2,1,0:T(8,128)(2,1)}, bf16[2,192,512]{2,1,0:T(8,128)(2,1)}, u32[]{:S(2)}, u32[]{:S(2)}) collective-permute-start(bf16[2,192,512]{2,1,0:T(8,128)(2,1)} %copy-done.25), channel_id=1, source_target_pairs={{0,16},{8,24},{16,0},{24,8},{1,17},{9,25},{17,1},{25,9},{2,18},{10... | collective-permute-start | bytes 1179656 | tf_op jit(solution)/shard_map/ppermute | solution.py:266
  310.3 48.5 %collective-permute-start.5 = (bf16[2,192,512]{2,1,0:T(8,128)(2,1)}, bf16[2,192,512]{2,1,0:T(8,128)(2,1)}, u32[]{:S(2)}, u32[]{:S(2)}) collective-permute-start(bf16[2,192,512]{2,1,0:T(8,128)(2,1)} %copy-done.24), channel_id=1, source_target_pairs={{0,24},{8,0},{16,8},{24,16},{1,25},{9,1},{17,9},{25,17},{2,26},{10... | collective-permute-start | bytes 1179656 | tf_op jit(solution)/shard_map/ppermute | solution.py:266
  311.6 51.9 %collective-permute-start = (bf16[2,192,512]{2,1,0:T(8,128)(2,1)}, bf16[2,192,512]{2,1,0:T(8,128)(2,1)}, u32[]{:S(2)}, u32[]{:S(2)}) collective-permute-start(bf16[2,192,512]{2,1,0:T(8,128)(2,1)} %copy-done.23), channel_id=1, source_target_pairs={{0,8},{8,16},{16,24},{24,0},{1,9},{9,17},{17,25},{25,1},{2,10},{10... | collective-permute-start | bytes 1179656 | tf_op jit(solution)/shard_map/ppermute | solution.py:266
  312.3 74.9 %collective-permute-start.1 = (bf16[2,192,512]{2,1,0:T(8,128)(2,1)}, bf16[2,192,512]{2,1,0:T(8,128)(2,1)}, u32[]{:S(2)}, u32[]{:S(2)}) collective-permute-start(bf16[2,192,512]{2,1,0:T(8,128)(2,1)} %copy-done.22), channel_id=1, source_target_pairs={{0,16},{8,24},{16,0},{24,8},{1,17},{9,25},{17,1},{25,9},{2,18},{10... | collective-permute-start | bytes 1179656 | tf_op jit(solution)/shard_map/ppermute | solution.py:266
  343.2 11.2 %copy-start.21 = (bf16[2,192,512]{2,1,0:T(8,128)(2,1)S(1)}, bf16[2,192,512]{2,1,0:T(8,128)(2,1)}, u32[]{:S(2)}) copy-start(bf16[2,192,512]{2,1,0:T(8,128)(2,1)} %copy-done.20) | copy-start | bytes 1179652
  343.2 15.6 %copy-start.13 = (bf16[2,192,512]{2,1,0:T(8,128)(2,1)S(1)}, bf16[2,192,512]{2,1,0:T(8,128)(2,1)}, u32[]{:S(2)}) copy-start(bf16[2,192,512]{2,1,0:T(8,128)(2,1)} %copy-done.12) | copy-start | bytes 1179652
  354.4 32.8 %collective-permute-start.2 = (bf16[2,192,512]{2,1,0:T(8,128)(2,1)S(1)}, bf16[2,192,512]{2,1,0:T(8,128)(2,1)S(1)}, u32[]{:S(2)}, u32[]{:S(2)}) collective-permute-start(bf16[2,192,512]{2,1,0:T(8,128)(2,1)S(1)} %copy-done.21), channel_id=1, source_target_pairs={{0,24},{8,0},{16,8},{24,16},{1,25},{9,1},{17,9},{25,17},{2,26},{10... | collective-permute-start | bytes 1179656 | tf_op jit(solution)/shard_map/ppermute | solution.py:266
  358.8 47.4 %collective-permute-start.6 = (bf16[2,192,512]{2,1,0:T(8,128)(2,1)S(1)}, bf16[2,192,512]{2,1,0:T(8,128)(2,1)S(1)}, u32[]{:S(2)}, u32[]{:S(2)}) collective-permute-start(bf16[2,192,512]{2,1,0:T(8,128)(2,1)S(1)} %get-tuple-element.42), channel_id=1, source_target_pairs={{0,8},{8,16},{16,24},{24,0},{1,9},{9,17},{17,25},{25,1},{2,10},{10... | collective-permute-start | bytes 1179656 | tf_op jit(solution)/shard_map/ppermute | solution.py:266
  360.3 61.2 %collective-permute-start.7 = (bf16[2,192,512]{2,1,0:T(8,128)(2,1)S(1)}, bf16[2,192,512]{2,1,0:T(8,128)(2,1)S(1)}, u32[]{:S(2)}, u32[]{:S(2)}) collective-permute-start(bf16[2,192,512]{2,1,0:T(8,128)(2,1)S(1)} %get-tuple-element.43), channel_id=1, source_target_pairs={{0,16},{8,24},{16,0},{24,8},{1,17},{9,25},{17,1},{25,9},{2,18},{10... | collective-permute-start | bytes 1179656 | tf_op jit(solution)/shard_map/ppermute | solution.py:266
  363.5 57.9 %collective-permute-start.8 = (bf16[2,192,512]{2,1,0:T(8,128)(2,1)S(1)}, bf16[2,192,512]{2,1,0:T(8,128)(2,1)S(1)}, u32[]{:S(2)}, u32[]{:S(2)}) collective-permute-start(bf16[2,192,512]{2,1,0:T(8,128)(2,1)S(1)} %get-tuple-element.44), channel_id=1, source_target_pairs={{0,24},{8,0},{16,8},{24,16},{1,25},{9,1},{17,9},{25,17},{2,26},{10... | collective-permute-start | bytes 1179656 | tf_op jit(solution)/shard_map/ppermute | solution.py:266
  387.2 50.5 %collective-permute-start.10 = (bf16[2,192,512]{2,1,0:T(8,128)(2,1)S(1)}, bf16[2,192,512]{2,1,0:T(8,128)(2,1)S(1)}, u32[]{:S(2)}, u32[]{:S(2)}) collective-permute-start(bf16[2,192,512]{2,1,0:T(8,128)(2,1)S(1)} %get-tuple-element.47), channel_id=1, source_target_pairs={{0,16},{8,24},{16,0},{24,8},{1,17},{9,25},{17,1},{25,9},{2,18},{10... | collective-permute-start | bytes 1179656 | tf_op jit(solution)/shard_map/ppermute | solution.py:266
  387.2 50.4 %collective-permute-start.11 = (bf16[2,192,512]{2,1,0:T(8,128)(2,1)S(1)}, bf16[2,192,512]{2,1,0:T(8,128)(2,1)S(1)}, u32[]{:S(2)}, u32[]{:S(2)}) collective-permute-start(bf16[2,192,512]{2,1,0:T(8,128)(2,1)S(1)} %get-tuple-element.48), channel_id=1, source_target_pairs={{0,24},{8,0},{16,8},{24,16},{1,25},{9,1},{17,9},{25,17},{2,26},{10... | collective-permute-start | bytes 1179656 | tf_op jit(solution)/shard_map/ppermute | solution.py:266
  406.2 31.5 %collective-permute-start.9 = (bf16[2,192,512]{2,1,0:T(8,128)(2,1)S(1)}, bf16[2,192,512]{2,1,0:T(8,128)(2,1)S(1)}, u32[]{:S(2)}, u32[]{:S(2)}) collective-permute-start(bf16[2,192,512]{2,1,0:T(8,128)(2,1)S(1)} %get-tuple-element.46), channel_id=1, source_target_pairs={{0,8},{8,16},{16,24},{24,0},{1,9},{9,17},{17,25},{25,1},{2,10},{10... | collective-permute-start | bytes 1179656 | tf_op jit(solution)/shard_map/ppermute | solution.py:266
